TPU v7x, 1024 devices: a whole 8x8x8 slice. The times are simulated.
1024 devices in a mesh: ep: 16 (over x, z_hi), edp: 64 (over z_lo, y, core).
Axes of the slice: x: 8, y: 8, z: 8 (z_hi: 2, z_lo: 4; z = z_hi * 4 + z_lo), core: 2. Of those that a mesh axis runs over, the one named last changes fastest.
Arguments:
- tokens: bfloat16 [2048, 4096], P('ep', 'edp'), may hold values from -6 to 6
- out_grad: bfloat16 [2048, 4096], P('ep', 'edp'), may hold values from -1.5 to 1.5
- probs: float32 [2048, 8], P('ep'), may hold values from 0.1 to 1
- expert_ids: int32 [2048, 8], P('ep'), may hold values from 0 to 127, all different within a row; in each aligned block of 128 rows (0 to 127, 128 to 255, ...) at most 16 rows name the same one
- w_gate: bfloat16 [64, 4096, 1024], P('edp', 'ep'), may hold values from -0.09375 to 0.09375
- w_up: bfloat16 [64, 4096, 1024], P('edp', 'ep'), may hold values from -0.09375 to 0.09375
- w_down: bfloat16 [64, 1024, 4096], P('edp', None, 'ep'), may hold values from -0.1875 to 0.1875
Outputs:
- token_grad: bfloat16 [2048, 4096], P('ep', 'edp')
- grad_gate: bfloat16 [64, 4096, 1024], P('edp', 'ep')
- grad_up: bfloat16 [64, 4096, 1024], P('edp', 'ep')
- grad_down: bfloat16 [64, 1024, 4096], P('edp', None, 'ep')
Inputs may be any that keep to these rules, and one draw needn't show every extreme that they name: `expert_ids`: each row names 8 different experts; within each context block of 128 tokens no expert is named by more than 16 tokens, a bound that some block reaches.
All inputs are finite; a program needn't handle non-finite values.
Results may differ from a plain program's by a relative error of at most 0.0058.
Values may be sent and summed in bfloat16 or wider, within the bound.
No kernel may reach another device: no remote copies, remote signals or barrier semaphores. Data moves between devices by JAX's collectives and lax.ppermute only.
A program may use at most 32 MiB of HBM per device.

v0:
```python
import jax
import jax.numpy as jnp
from jax import lax
from jax.sharding import PartitionSpec as P

CAP = 16


def swiglu_back(gate_sum, up_sum, back_sum, weight_col):
    sigmoid_gate = jax.nn.sigmoid(gate_sum)
    silu_gate = gate_sum * sigmoid_gate
    hidden_grad = weight_col * back_sum
    hidden_weighted = (weight_col * silu_gate * up_sum).astype(jnp.bfloat16)
    up_grad = (hidden_grad * silu_gate).astype(jnp.bfloat16)
    gate_grad = (
        hidden_grad * up_sum * sigmoid_gate * (1.0 + gate_sum * (1.0 - sigmoid_gate))
    ).astype(jnp.bfloat16)
    return (gate_grad, up_grad, hidden_weighted)


def per_device(tokens, out_grad, probs, expert_ids, w_gate, w_up, w_down):
    tok_rows = tokens.shape[0]
    picks_each = expert_ids.shape[1]
    windows = lax.axis_size("edp")
    capacity = CAP
    slot_total = windows * capacity
    flat_ids = expert_ids.reshape(-1)
    flat_probs = probs.reshape(-1)
    onehot_ids = (flat_ids[:, None] == jnp.arange(windows, dtype=jnp.int32)[None, :]).astype(
        jnp.int32
    )
    ranking = jnp.sum((jnp.cumsum(onehot_ids, axis=0) - onehot_ids) * onehot_ids, axis=1)
    inside = jnp.sum(onehot_ids, axis=1)
    slot_code = jnp.where(inside > 0, flat_ids * capacity + ranking, -1)
    matches = slot_code[:, None] == jnp.arange(slot_total, dtype=jnp.int32)[None, :]
    per_token = jnp.any(matches.reshape(tok_rows, picks_each, slot_total), axis=1)
    dispatch_matrix = per_token.T.astype(jnp.bfloat16)
    slot_weights = jnp.sum(jnp.where(matches, flat_probs[:, None], 0.0), axis=0)
    my_expert = lax.axis_index("edp")
    share_weight = lax.dynamic_slice_in_dim(slot_weights, my_expert * capacity, capacity, 0)
    tok_block = jnp.dot(dispatch_matrix, tokens, preferred_element_type=jnp.float32).astype(
        jnp.bfloat16
    )
    grad_block = jnp.dot(dispatch_matrix, out_grad, preferred_element_type=jnp.float32).astype(
        jnp.bfloat16
    )
    tok_block = tok_block.reshape(windows, capacity, tokens.shape[1])
    grad_block = grad_block.reshape(windows, capacity, tokens.shape[1])
    slot_tokens, slot_grads = (
        lax.all_to_all(
            lax.all_to_all(tok_block, "edp", split_axis=0, concat_axis=2, tiled=True),
            "ep",
            split_axis=2,
            concat_axis=1,
            tiled=True,
        ),
        lax.all_to_all(
            lax.all_to_all(grad_block, "edp", split_axis=0, concat_axis=2, tiled=True),
            "ep",
            split_axis=2,
            concat_axis=1,
            tiled=True,
        ),
    )
    slot_tokens = slot_tokens[0]
    slot_grads = slot_grads[0]
    gate_local = w_gate[0]
    up_local = w_up[0]
    down_local = w_down[0]
    hidden_units = gate_local.shape[1]
    contract_last = (((1,), (1,)), ((), ()))
    summed = lax.psum_scatter(
        jnp.concatenate(
            [
                jnp.dot(slot_tokens, gate_local, preferred_element_type=jnp.float32),
                jnp.dot(slot_tokens, up_local, preferred_element_type=jnp.float32),
                lax.dot_general(
                    slot_grads, down_local, contract_last, preferred_element_type=jnp.float32
                ),
            ],
            axis=1,
        ),
        "ep",
        scatter_dimension=0,
        tiled=True,
    )
    gate_sum = summed[:, :hidden_units]
    up_sum = summed[:, hidden_units : 2 * hidden_units]
    back_sum = summed[:, 2 * hidden_units :]
    gate_grad, up_grad, hidden_weighted = swiglu_back(
        gate_sum, up_sum, back_sum, share_weight[:, None]
    )
    gate_grad, up_grad, hidden_weighted = (
        lax.all_gather(gate_grad, "ep", axis=0, tiled=True),
        lax.all_gather(up_grad, "ep", axis=0, tiled=True),
        lax.all_gather(hidden_weighted, "ep", axis=0, tiled=True),
    )
    slot_grad = (
        lax.dot_general(gate_grad, gate_local, contract_last, preferred_element_type=jnp.float32)
        + lax.dot_general(up_grad, up_local, contract_last, preferred_element_type=jnp.float32)
    ).astype(jnp.bfloat16)
    contract_first = (((0,), (0,)), ((), ()))
    grad_gate = lax.dot_general(
        slot_tokens, gate_grad, contract_first, preferred_element_type=jnp.float32
    ).astype(jnp.bfloat16)
    grad_up = lax.dot_general(
        slot_tokens, up_grad, contract_first, preferred_element_type=jnp.float32
    ).astype(jnp.bfloat16)
    grad_down = lax.dot_general(
        hidden_weighted, slot_grads, contract_first, preferred_element_type=jnp.float32
    ).astype(jnp.bfloat16)
    returned = lax.all_to_all(
        lax.all_to_all(slot_grad[None], "ep", split_axis=1, concat_axis=2, tiled=True),
        "edp",
        split_axis=2,
        concat_axis=0,
        tiled=True,
    )
    returned = returned.reshape(slot_total, tokens.shape[1])
    token_grad = lax.dot_general(
        dispatch_matrix, returned, contract_first, preferred_element_type=jnp.float32
    ).astype(jnp.bfloat16)
    return (token_grad, grad_gate[None], grad_up[None], grad_down[None])


def solution(mesh):
    placed = (
        P("ep", "edp"),
        P("ep", "edp"),
        P("ep", None),
        P("ep", None),
        P("edp", "ep", None),
        P("edp", "ep", None),
        P("edp", None, "ep"),
    )
    return jax.shard_map(
        per_device,
        mesh=mesh,
        in_specs=placed,
        out_specs=(
            P("ep", "edp"),
            P("edp", "ep", None),
            P("edp", "ep", None),
            P("edp", None, "ep"),
        ),
        check_vma=False,
    )
```

profile of v0, /device:TPU:1, one launch (start us, length us, event | category | flops | bytes accessed | tf_op | source)
XLA Modules:
  0.0 648.7 jit_solution(12293460059729568361)
XLA Ops:
  7.2 0.8 copy.88
  8.3 18.0 %reduce-window.6 = s32[64,8,128]{2,1,0:T(8,128)S(1)} reduce-window(s32[64,8,128]{2,1,0:T(8,128)S(1)} %fusion.17, s32[]{:T(128)} %constant.8.clone.1), window={size=1x1x128 pad=0_0x0_0x127_0}, to_apply=%region_1.2 | reduce-window | flops 8323072 | bytes 524292 | tf_op jit(solution)/shard_map/reduce-window
  26.3 0.1 slice.20
  26.4 0.1 copy.90
  26.7 0.1 broadcast_add_fusion
  27.2 0.7 add_select_fusion.1
  28.1 1.3 fusion
  29.4 0.2 convolution_convert_fusion.4
  29.6 0.2 copy.96
  29.8 0.8 reshape.73
  30.6 18.2 %all-to-all-start = ((bf16[64,2,512]{2,1,0:T(2,128)(2,1)}), bf16[64,2,512]{2,1,0:T(2,128)(2,1)S(1)}, u32[]{:S(2)}, u32[]{:S(2)}) async-start(bf16[64,2,512]{2,1,0:T(2,128)(2,1)} %reshape.73), calls=%async_computation | async-start | bytes 262144 | tf_op jit(solution)/shard_map/all_to_all | solution.py:51
  48.9 0.2 convolution_convert_fusion.3
  49.1 0.2 copy.101
  49.2 0.8 reshape.69
  50.1 8.9 %all-to-all-done = bf16[64,2,512]{2,1,0:T(2,128)(2,1)S(1)} async-done(((bf16[64,2,512]{2,1,0:T(2,128)(2,1)}), bf16[64,2,512]{2,1,0:T(2,128)(2,1)S(1)}, u32[]{:S(2)}, u32[]{:S(2)}) %all-to-all-start) | async-done | bytes 131104 | tf_op jit(solution)/shard_map/all_to_all | solution.py:51
  59.0 4.9 all-to-all-start.2
  63.9 0.2 reshape.74
  64.2 0.3 all_to_all.75
  64.5 2.7 copy.98
  67.2 0.5 broadcast.51
  67.8 23.4 %reduce.1 = bf16[4096,16]{1,0:T(8,128)(2,1)} reduce(bf16[4096,1,16]{2,1,0:T(2,128)(2,1)S(1)} %bitcast.95, bf16[]{:T(256)} %broadcast.51), dimensions={1}, to_apply=%bitcast.68.reduce_sub_computation | reduce | bytes 262146
  91.2 3.1 reshape.75
  94.3 15.4 %all-to-all-start.1 = ((bf16[16,2,2048]{2,1,0:T(2,128)(2,1)}), bf16[16,2,2048]{2,1,0:T(2,128)(2,1)S(1)}, u32[]{:S(2)}, u32[]{:S(2)}) async-start(bf16[16,2,2048]{2,1,0:T(2,128)(2,1)} %reshape.75), calls=%async_computation.1 | async-start | bytes 262144 | tf_op jit(solution)/shard_map/all_to_all | solution.py:50
  109.7 0.2 reshape.70
  110.0 0.3 all_to_all.82
  110.3 2.7 copy.103
  113.0 23.4 %reduce = bf16[4096,16]{1,0:T(8,128)(2,1)} reduce(bf16[4096,1,16]{2,1,0:T(2,128)(2,1)S(1)} %bitcast.97, bf16[]{:T(256)} %broadcast.51), dimensions={1}, to_apply=%bitcast.66.reduce_sub_computation | reduce | bytes 262146
  136.4 3.2 reshape.71
  139.6 11.5 %all-to-all-start.3 = ((bf16[16,2,2048]{2,1,0:T(2,128)(2,1)}), bf16[16,2,2048]{2,1,0:T(2,128)(2,1)S(1)}, u32[]{:S(2)}, u32[]{:S(2)}) async-start(bf16[16,2,2048]{2,1,0:T(2,128)(2,1)} %reshape.71), calls=%async_computation.3 | async-start | bytes 262144 | tf_op jit(solution)/shard_map/all_to_all | solution.py:57
  151.1 1.8 reshape.76
  152.9 2.0 copy.99
  155.0 1.3 fusion.9
  156.3 1.3 fusion.13
  157.7 5.8 all-to-all-done.3
  163.4 1.8 reshape.72
  165.3 2.0 copy.104
  167.4 1.5 fusion.6
  169.0 2.0 pad_maximum_fusion
  171.0 0.7 copy-done.6
  171.8 0.6 select_reduce_fusion
  172.5 232.5 %reduce-scatter.2.cloned.1.call-done = f32[16,3072]{1,0:T(8,128)} async-done(((f32[256,3072]{1,0:T(8,128)}), f32[16,3072]{1,0:T(8,128)}) %reduce-scatter.2.cloned.1.call-update) | async-done | bytes 196624 | tf_op jit(solution)/shard_map/reduce_scatter | solution.py:72
  404.9 1.0 multiply_convert_fusion
  405.9 43.2 %all_gather.9 = bf16[256,1024]{1,0:T(8,128)(2,1)S(1)} all-gather(bf16[16,1024]{1,0:T(8,128)(2,1)S(1)} %get-tuple-element.9), channel_id=1, replica_groups=mesh['ep'=16,'edp'=64] {'ep'}, dimensions={0}, use_global_device_ids=true | all-gather | bytes 557056 | tf_op jit(solution)/shard_map/all_gather | solution.py:94
  449.1 0.3 fusion.11
  449.4 1.1 fusion.1
  450.5 51.1 %all_gather.10 = bf16[256,1024]{1,0:T(8,128)(2,1)S(1)} all-gather(bf16[16,1024]{1,0:T(8,128)(2,1)S(1)} %get-tuple-element.10), channel_id=1, replica_groups=mesh['ep'=16,'edp'=64] {'ep'}, dimensions={0}, use_global_device_ids=true | all-gather | bytes 557056 | tf_op jit(solution)/shard_map/all_gather | solution.py:95
  501.6 0.3 fusion.5
  502.0 0.2 copy.118
  502.2 1.4 reduce.2
  503.6 0.7 reshape.77
  504.3 3.5 all-to-all-start.4
  507.8 53.3 %all_gather.11 = bf16[256,1024]{1,0:T(8,128)(2,1)} all-gather(bf16[16,1024]{1,0:T(8,128)(2,1)S(1)} %get-tuple-element.8), channel_id=1, replica_groups=mesh['ep'=16,'edp'=64] {'ep'}, dimensions={0}, use_global_device_ids=true | all-gather | bytes 557056 | tf_op jit(solution)/shard_map/all_gather | solution.py:96
  561.3 2.7 copy.108
  564.0 23.4 %reduce.3 = bf16[4096,16]{1,0:T(8,128)(2,1)} reduce(bf16[4096,1,16]{2,1,0:T(2,128)(2,1)S(1)} %bitcast.96, bf16[]{:T(256)} %broadcast.51), dimensions={1}, to_apply=%bitcast.72.reduce_sub_computation | reduce | bytes 262146
  587.4 3.1 reshape.79
  590.6 36.1 %all-to-all-start.5 = ((bf16[64,2,512]{2,1,0:T(2,128)(2,1)}), bf16[64,2,512]{2,1,0:T(2,128)(2,1)S(1)}, u32[]{:S(2)}, u32[]{:S(2)}) async-start(bf16[64,2,512]{2,1,0:T(2,128)(2,1)} %reshape.79), calls=%async_computation.6 | async-start | bytes 262144 | tf_op jit(solution)/shard_map/all_to_all | solution.py:112
  626.7 1.1 fusion.2
  627.8 2.2 fusion.3
  630.0 6.7 %all-to-all-done.5 = bf16[64,2,512]{2,1,0:T(2,128)(2,1)S(1)} async-done(((bf16[64,2,512]{2,1,0:T(2,128)(2,1)}), bf16[64,2,512]{2,1,0:T(2,128)(2,1)S(1)}, u32[]{:S(2)}, u32[]{:S(2)}) %all-to-all-start.5) | async-done | bytes 131104 | tf_op jit(solution)/shard_map/all_to_all | solution.py:112
  636.8 1.8 reshape.80
  638.6 2.0 copy.109
  640.6 0.2 all_to_all.91
  640.8 0.2 copy.110
  641.0 0.9 convolution_convert_fusion.5
  (49 shorter events, 1.7 us)
Async XLA Ops:
  7.2 149.2 %copy-start = (bf16[1,256,1024]{2,1,0:T(8,128)(2,1)S(1)}, bf16[1,256,1024]{2,1,0:T(8,128)(2,1)}, u32[]{:S(2)}) copy-start(bf16[1,256,1024]{2,1,0:T(8,128)(2,1)} %param.11) | copy-start | bytes 1572868
  7.2 22.2 %copy-start.7 = (bf16[128,64]{0,1:T(8,128)(2,1)S(1)}, bf16[128,64]{0,1:T(8,128)(2,1)}, u32[]{:S(2)}) copy-start(bf16[128,64]{0,1:T(8,128)(2,1)} %param.7) | copy-start | bytes 49156
  7.2 41.7 %copy-start.8 = (bf16[128,64]{0,1:T(8,128)(2,1)S(1)}, bf16[128,64]{0,1:T(8,128)(2,1)}, u32[]{:S(2)}) copy-start(bf16[128,64]{0,1:T(8,128)(2,1)} %param.8) | copy-start | bytes 49156
  29.4 34.8 %copy-start.4 = (pred[128,1024]{1,0:T(8,128)(4,1)}, pred[128,1024]{1,0:T(8,128)(4,1)S(1)}, u32[]{:S(2)}) copy-start(pred[128,1024]{1,0:T(8,128)(4,1)S(1)} %fusion) | copy-start | bytes 393220
  30.6 28.4 %all-to-all-start = ((bf16[64,2,512]{2,1,0:T(2,128)(2,1)}), bf16[64,2,512]{2,1,0:T(2,128)(2,1)S(1)}, u32[]{:S(2)}, u32[]{:S(2)}) async-start(bf16[64,2,512]{2,1,0:T(2,128)(2,1)} %reshape.73), calls=%async_computation | async-start | bytes 262144 | tf_op jit(solution)/shard_map/all_to_all | solution.py:51
  59.0 35.2 %all-to-all-start.2 = ((bf16[64,2,512]{2,1,0:T(2,128)(2,1)}), bf16[64,2,512]{2,1,0:T(2,128)(2,1)S(1)}, u32[]{:S(2)}, u32[]{:S(2)}) async-start(bf16[64,2,512]{2,1,0:T(2,128)(2,1)} %reshape.69), calls=%async_computation.2 | async-start | bytes 262144 | tf_op jit(solution)/shard_map/all_to_all | solution.py:58
  94.3 45.3 %all-to-all-start.1 = ((bf16[16,2,2048]{2,1,0:T(2,128)(2,1)}), bf16[16,2,2048]{2,1,0:T(2,128)(2,1)S(1)}, u32[]{:S(2)}, u32[]{:S(2)}) async-start(bf16[16,2,2048]{2,1,0:T(2,128)(2,1)} %reshape.75), calls=%async_computation.1 | async-start | bytes 262144 | tf_op jit(solution)/shard_map/all_to_all | solution.py:50
  136.4 18.6 %copy-start.3 = (bf16[1,256,1024]{2,1,0:T(8,128)(2,1)S(1)}, bf16[1,256,1024]{2,1,0:T(8,128)(2,1)}, u32[]{:S(2)}) copy-start(bf16[1,256,1024]{2,1,0:T(8,128)(2,1)} %param.12) | copy-start | bytes 1572868
  139.6 23.9 %all-to-all-start.3 = ((bf16[16,2,2048]{2,1,0:T(2,128)(2,1)}), bf16[16,2,2048]{2,1,0:T(2,128)(2,1)S(1)}, u32[]{:S(2)}, u32[]{:S(2)}) async-start(bf16[16,2,2048]{2,1,0:T(2,128)(2,1)} %reshape.71), calls=%async_computation.3 | async-start | bytes 262144 | tf_op jit(solution)/shard_map/all_to_all | solution.py:57
  151.1 253.9 %reduce-scatter.2.cloned.1.call-start = ((), (), s32[]{:S(2)}) async-start(), calls=%async_computation.7 | async-start | bytes 3342336 | tf_op jit(solution)/shard_map/reduce_scatter | solution.py:72
  167.2 1.6 copy-start.1
  167.3 1.7 copy-start.2
  171.0 0.7 copy-start.6
  504.3 56.8 %all-to-all-start.4 = ((bf16[16,2,2048]{2,1,0:T(2,128)(2,1)}), bf16[16,2,2048]{2,1,0:T(2,128)(2,1)S(1)}, u32[]{:S(2)}, u32[]{:S(2)}) async-start(bf16[16,2,2048]{2,1,0:T(2,128)(2,1)} %reshape.77), calls=%async_computation.5 | async-start | bytes 262144 | tf_op jit(solution)/shard_map/all_to_all | solution.py:113
  590.6 46.2 %all-to-all-start.5 = ((bf16[64,2,512]{2,1,0:T(2,128)(2,1)}), bf16[64,2,512]{2,1,0:T(2,128)(2,1)S(1)}, u32[]{:S(2)}, u32[]{:S(2)}) async-start(bf16[64,2,512]{2,1,0:T(2,128)(2,1)} %reshape.79), calls=%async_computation.6 | async-start | bytes 262144 | tf_op jit(solution)/shard_map/all_to_all | solution.py:112
  627.8 13.2 %copy-start.5 = (pred[128,1024]{1,0:T(8,128)(4,1)S(1)}, pred[128,1024]{1,0:T(8,128)(4,1)}, u32[]{:S(2)}) copy-start(pred[128,1024]{1,0:T(8,128)(4,1)} %copy-done.4) | copy-start | bytes 393220
Sparse Core Ops, SparseCore 0:
  171.1 233.7 reduce-scatter.1
where the time goes:
time: 650 us; the launch traced here: 649 us
  waiting for transfers between devices  254 us (39%)
  blocking collectives  148 us (23%)
  other arithmetic  95.5 us (15%)
  starting transfers between devices  89.6 us (14%)
  local copies, waits for them, and re-layouts  37.1 us (6%)
  between operations  14.5 us (2%)
  matrix products  10.5 us (2%)
    reduce_scatter x1, waiting for transfers between devices, per_device(): lax.psum_scatter(jnp.concatenate([jnp.dot(slot_tokens, gate_local, prefer...  232 us
    unnamed x4, other arithmetic  71.6 us
    all_gather x1, blocking collectives, per_device(): lax.all_gather(hidden_weighted, 'ep', axis=0, tiled=True)  53.3 us
    all_gather x1, blocking collectives, per_device(): lax.all_gather(up_grad, 'ep', axis=0, tiled=True)  51.1 us
    all_gather x1, blocking collectives, per_device(): lax.all_gather(gate_grad, 'ep', axis=0, tiled=True)  43.2 us
    all_to_all x1, starting transfers between devices, per_device(): lax.all_to_all(lax.all_to_all(slot_grad[None], 'ep', split_axis=1, concat...  36.1 us
    unnamed x36, local copies, waits for them, and re-layouts  20 us
    all_to_all x1, starting transfers between devices, per_device(): lax.all_to_all(tok_block, 'edp', split_axis=0, concat_axis=2, tiled=True)  18.2 us
  transfers between devices with their start and end apart: 7, of which 4 were waited for; matrix products, arithmetic and copies ran while one was open for 11% of the time, Pallas kernels for 0%

commit v1 on v0

v1 whole, which is shorter than its diff:
```python
import jax
import jax.numpy as jnp
from jax import lax
from jax.experimental import pallas as pl
from jax.experimental.pallas import tpu as pltpu
from jax.sharding import PartitionSpec as P

CAP = 16
BF16 = jnp.bfloat16
F32 = jnp.float32
LAST = (((1,), (1,)), ((), ()))
FIRST = (((0,), (0,)), ((), ()))


def call(body, outs, flops, moved, *args):
    return pl.pallas_call(
        body,
        out_shape=outs,
        compiler_params=pltpu.CompilerParams(vmem_limit_bytes=40 * 1024 * 1024),
        cost_estimate=pl.CostEstimate(flops=flops, bytes_accessed=moved, transcendentals=0),
    )(*args)


def arr(shape, dtype=BF16):
    return jax.ShapeDtypeStruct(shape, dtype)


def before(toks):
    row = lax.broadcasted_iota(jnp.int32, (toks, toks), 0)
    col = lax.broadcasted_iota(jnp.int32, (toks, toks), 1)
    return jnp.where(row < col, 1.0, 0.0).astype(BF16)


def dispatch_body(experts, packed_ref, sent_ref, disp_ref):
    feats = packed_ref[0:128, :]
    ids = packed_ref[128:144, :].astype(F32)
    toks = ids.shape[1]
    names = lax.broadcasted_iota(jnp.int32, (experts, toks), 0).astype(F32)
    mask = jnp.zeros((experts, toks), F32)
    for k in range(8):
        mask = mask + jnp.where(ids[k : k + 1, :] == names, 1.0, 0.0)
    rank = jnp.dot(mask.astype(BF16), before(toks), preferred_element_type=F32)
    slot = jnp.where(mask > 0.0, rank, -1.0)
    place = lax.broadcasted_iota(jnp.int32, (CAP, toks), 0).astype(F32)
    for e in range(experts):
        disp_ref[e * CAP : (e + 1) * CAP, :] = jnp.where(
            slot[e : e + 1, :] == place, 1.0, 0.0
        ).astype(BF16)
    sent_ref[...] = lax.dot_general(
        disp_ref[...], feats, LAST, preferred_element_type=F32
    ).astype(BF16)


def weight_body(mine_ref, probs_ref, out_ref):
    mine = mine_ref[...]
    toks = mine.shape[1]
    mask = jnp.sum(mine, axis=0, keepdims=True)
    weight = jnp.sum(mine * probs_ref[...], axis=0, keepdims=True)
    rank = jnp.dot(
        jnp.broadcast_to(mask, (16, toks)).astype(BF16), before(toks), preferred_element_type=F32
    )
    place = lax.broadcasted_iota(jnp.int32, (CAP, toks), 0).astype(F32)
    hit = (rank == place) & (jnp.broadcast_to(mask, (CAP, toks)) > 0.0)
    picked = jnp.where(hit, jnp.broadcast_to(weight, (CAP, toks)), 0.0)
    out_ref[...] = jnp.broadcast_to(jnp.sum(picked, axis=1, keepdims=True), (CAP, toks))


def project_body(recv_ref, gate_ref, up_ref, down_ref, part_ref, x_ref, y_ref):
    rows = recv_ref.shape[0] // 4
    for q in range(4):
        block = recv_ref[q * rows : (q + 1) * rows, :]
        x_ref[:, q * 64 : (q + 1) * 64] = block[:, :64]
        y_ref[:, q * 64 : (q + 1) * 64] = block[:, 64:]
    x = x_ref[...]
    y = y_ref[...]
    hid = gate_ref.shape[1]
    part_ref[:, 0:hid] = jnp.dot(x, gate_ref[...], preferred_element_type=F32).astype(BF16)
    part_ref[:, hid : 2 * hid] = jnp.dot(x, up_ref[...], preferred_element_type=F32).astype(BF16)
    part_ref[:, 2 * hid : 3 * hid] = lax.dot_general(
        y, down_ref[...], LAST, preferred_element_type=F32
    ).astype(BF16)


def hidden_body(parts_ref, weight_ref, grads_ref, weighted_ref):
    peers = parts_ref.shape[0] // CAP
    hid = parts_ref.shape[1] // 3
    total = parts_ref[0:CAP, :].astype(F32)
    for s in range(1, peers):
        total = total + parts_ref[s * CAP : (s + 1) * CAP, :].astype(F32)
    gate = total[:, 0:hid]
    up = total[:, hid : 2 * hid]
    back = total[:, 2 * hid : 3 * hid]
    weight = weight_ref[:, 0:1]
    sig = jax.nn.sigmoid(gate)
    silu = gate * sig
    hidden_grad = weight * back
    hidden_weighted = (weight * silu * up).astype(BF16)
    up_grad = (hidden_grad * silu).astype(BF16)
    gate_grad = (hidden_grad * up * sig * (1.0 + gate * (1.0 - sig))).astype(BF16)
    for s in range(peers):
        rows = slice(s * CAP, (s + 1) * CAP)
        grads_ref[rows, 0:hid] = gate_grad
        grads_ref[rows, hid : 2 * hid] = up_grad
        weighted_ref[rows, :] = hidden_weighted


def slot_grad_body(grads_ref, gate_ref, up_ref, out_ref):
    hid = gate_ref.shape[1]
    slot_grad = lax.dot_general(
        grads_ref[:, 0:hid], gate_ref[...], LAST, preferred_element_type=F32
    ) + lax.dot_general(
        grads_ref[:, hid : 2 * hid], up_ref[...], LAST, preferred_element_type=F32
    )
    rows = slot_grad.shape[0]
    pairs = slot_grad.reshape(rows // 16, 2, 8, slot_grad.shape[1])
    low = pairs[:, 0].reshape(rows // 2, slot_grad.shape[1])
    high = pairs[:, 1].reshape(rows // 2, slot_grad.shape[1])
    for q in range(4):
        cols = slice(q * 64, (q + 1) * 64)
        out_ref[q * (rows // 2) : (q + 1) * (rows // 2), :] = jnp.concatenate(
            [low[:, cols], high[:, cols]], axis=1
        ).astype(BF16)


def weight_grads_body(x_ref, grads_ref, gate_ref, up_ref):
    hid = gate_ref.shape[1]
    x = x_ref[...]
    gate_ref[...] = lax.dot_general(
        x, grads_ref[:, 0:hid], FIRST, preferred_element_type=F32
    ).astype(BF16)
    up_ref[...] = lax.dot_general(
        x, grads_ref[:, hid : 2 * hid], FIRST, preferred_element_type=F32
    ).astype(BF16)


def down_grad_body(weighted_ref, y_ref, out_ref):
    out_ref[...] = lax.dot_general(
        weighted_ref[...], y_ref[...], FIRST, preferred_element_type=F32
    ).astype(BF16)


def combine_body(recv_ref, disp_ref, out_ref):
    rows = disp_ref.shape[0]
    toks = disp_ref.shape[1]
    disp = disp_ref[...].astype(F32).reshape(rows // 16, 2, 8, toks)
    low = disp[:, 0].reshape(rows // 2, toks).astype(BF16)
    high = disp[:, 1].reshape(rows // 2, toks).astype(BF16)
    recv = recv_ref[...]
    out = lax.dot_general(recv, low, FIRST, preferred_element_type=F32)[0:64, :]
    out = out + lax.dot_general(recv, high, FIRST, preferred_element_type=F32)[64:128, :]
    out_ref[...] = out.astype(BF16)


def per_device(tokens, out_grad, probs, expert_ids, w_gate, w_up, w_down):
    blocks = lax.axis_size("ep")
    experts = lax.axis_size("edp")
    toks, width = tokens.shape
    share = experts // blocks
    slots = blocks * CAP
    wide = w_gate.shape[1]
    hid = w_gate.shape[2]
    gate, up, down = w_gate[0], w_up[0], w_down[0]

    there = [
        (b * experts + j, (j // share) * experts + (j % share) * blocks + b)
        for b in range(blocks)
        for j in range(experts)
    ]
    back = [(d, s) for s, d in there]

    ids = expert_ids.T
    packed = jnp.concatenate(
        [tokens.T, out_grad.T, ids.astype(BF16), jnp.zeros((8, toks), BF16)], axis=0
    )
    packed = lax.ppermute(packed, ("ep", "edp"), there)

    mine = (ids == lax.axis_index("edp")).astype(F32)
    weight = call(weight_body, arr((CAP, toks), F32), 10**5, 10**4, mine, probs.T)

    def body(*refs):
        dispatch_body(experts, *refs)

    sent, disp = call(
        body,
        (arr((experts * CAP, 2 * width)), arr((experts * CAP, toks))),
        2 * experts * CAP * toks * 2 * width,
        6 * 10**5,
        packed,
    )
    recv = lax.all_to_all(
        sent.reshape(experts, CAP, 2 * width), "edp", split_axis=0, concat_axis=0, tiled=True
    ).reshape(experts * CAP, 2 * width)

    part, x_s, y_s = call(
        project_body,
        (arr((slots, 3 * hid)), arr((slots, wide)), arr((slots, wide))),
        6 * slots * wide * hid,
        4 * 10**6,
        recv,
        gate,
        up,
        down,
    )
    parts = lax.all_to_all(
        part.reshape(blocks, CAP, 3 * hid), "ep", split_axis=0, concat_axis=0, tiled=True
    ).reshape(slots, 3 * hid)

    grads, weighted = call(
        hidden_body,
        (arr((slots, 2 * hid)), arr((slots, hid))),
        10**6,
        3 * 10**6,
        parts,
        weight,
    )
    grads = lax.all_to_all(
        grads.reshape(blocks, CAP, 2 * hid), "ep", split_axis=0, concat_axis=0, tiled=True
    ).reshape(slots, 2 * hid)
    weighted = lax.all_to_all(
        weighted.reshape(blocks, CAP, hid), "ep", split_axis=0, concat_axis=0, tiled=True
    ).reshape(slots, hid)

    slot_grad = call(
        slot_grad_body,
        arr((4 * slots // 2, 128)),
        4 * slots * wide * hid,
        2 * 10**6,
        grads,
        gate,
        up,
    )
    returned = lax.all_to_all(
        slot_grad.reshape(experts, 8, 128), "edp", split_axis=0, concat_axis=0, tiled=True
    ).reshape(experts * 8, 128)

    grad_gate, grad_up = call(
        weight_grads_body,
        (arr((wide, hid)), arr((wide, hid))),
        4 * slots * wide * hid,
        2 * 10**6,
        x_s,
        grads,
    )
    grad_down = call(
        down_grad_body, arr((hid, wide)), 2 * slots * wide * hid, 10**6, weighted, y_s
    )
    token_grad = call(
        combine_body, arr((width, toks)), 4 * experts * 8 * 128 * toks, 4 * 10**5, returned, disp
    )
    token_grad = lax.ppermute(token_grad, ("ep", "edp"), back).T
    return (token_grad, grad_gate[None], grad_up[None], grad_down[None])


def solution(mesh):
    placed = (
        P("ep", "edp"),
        P("ep", "edp"),
        P("ep", None),
        P("ep", None),
        P("edp", "ep", None),
        P("edp", "ep", None),
        P("edp", None, "ep"),
    )
    return jax.shard_map(
        per_device,
        mesh=mesh,
        in_specs=placed,
        out_specs=(
            P("ep", "edp"),
            P("edp", "ep", None),
            P("edp", "ep", None),
            P("edp", None, "ep"),
        ),
        check_vma=False,
    )
```

time: 650 us -> 221 us (0.34)
  the two profiles are of different devices: /device:TPU:1 before, /device:TPU:44 now
where the time goes in v1:
time: 221 us; the launch traced here: 220 us
  waiting for transfers between devices  86.5 us (39%)
  blocking collectives  69.1 us (31%)
  starting transfers between devices  50.9 us (23%)
  Pallas kernels  7.5 us (3%)
  local copies, waits for them, and re-layouts  3.82 us (2%)
    all_to_all x1, waiting for transfers between devices, per_device(): lax.all_to_all(part.reshape(blocks, CAP, 3 * hid), 'ep', split_axis=0, co...  53.4 us
    all_to_all x1, blocking collectives, per_device(): lax.all_to_all(grads.reshape(blocks, CAP, 2 * hid), 'ep', split_axis=0, c...  43.5 us
    all_to_all x1, blocking collectives, per_device(): lax.all_to_all(sent.reshape(experts, CAP, 2 * width), 'edp', split_axis=0...  25.6 us
    ppermute x1, starting transfers between devices, per_device(): packed = lax.ppermute(packed, ('ep', 'edp'), there)  18.3 us
    all_to_all x1, waiting for transfers between devices, per_device(): lax.all_to_all(weighted.reshape(blocks, CAP, hid), 'ep', split_axis=0, co...  15.2 us
    all_to_all x1, starting transfers between devices, per_device(): lax.all_to_all(part.reshape(blocks, CAP, 3 * hid), 'ep', split_axis=0, co...  12.3 us
    ppermute x1, waiting for transfers between devices, per_device(): token_grad = lax.ppermute(token_grad, ('ep', 'edp'), back).T  8.19 us
    all_to_all x1, waiting for transfers between devices, per_device(): lax.all_to_all(slot_grad.reshape(experts, 8, 128), 'edp', split_axis=0, c...  8.02 us
  transfers between devices with their start and end apart: 5, of which 5 were waited for; matrix products, arithmetic and copies ran while one was open for 0% of the time, Pallas kernels for 2%

profile of v1, /device:TPU:44, one launch (start us, length us, event | category | flops | bytes accessed | tf_op | source)
XLA Modules:
  0.0 220.0 jit_solution(1094824818678043721)
XLA Ops:
  0.6 0.7 convert_bitcast_fusion.1
  1.3 0.1 pad.3.clone
  1.4 0.8 maximum_maximum_fusion
  2.2 18.3 %collective-permute-start = (bf16[144,128]{1,0:T(8,128)(2,1)S(1)}, bf16[144,128]{1,0:T(8,128)(2,1)S(1)}, u32[]{:S(2)}, u32[]{:S(2)}) collective-permute-start(bf16[144,128]{1,0:T(8,128)(2,1)S(1)} %maximum_maximum_fusion), channel_id=1, source_target_pairs={{0,0},{1,16},{2,32},{3,48},{4,64},{5,80},{6,96},{7,112},{8,128},{9... | collective-permute-start | bytes 110600 | tf_op jit(solution)/shard_map/ppermute | solution.py:175
  20.5 1.6 collective-permute-done.refs_0_
  22.2 0.4 shard_map.102
  22.5 25.6 %all_to_all.25 = bf16[64,16,128]{2,1,0:T(8,128)(2,1)S(1)} all-to-all(bf16[64,16,128]{2,1,0:T(8,128)(2,1)S(1)} %bitcast.36), channel_id=1, replica_groups=mesh['ep'=16,'edp'=64] {'edp'}, dimensions={0} | all-to-all | bytes 524288 | tf_op jit(solution)/shard_map/all_to_all | solution.py:190
  48.1 0.0 copy-start
  48.1 1.0 copy-done
  49.1 0.0 copy-start.2
  49.1 1.0 copy-done.2
  50.2 0.0 copy-start.4
  50.2 1.0 copy-done.4
  51.2 1.8 shard_map.103
  53.0 0.0 copy-start.6
  53.0 0.0 copy-start.5
  53.0 12.3 %all-to-all-start.1 = ((bf16[16,16,3072]{2,1,0:T(8,128)(2,1)}), bf16[16,16,3072]{2,1,0:T(8,128)(2,1)S(1)}, u32[]{:S(2)}, u32[]{:S(2)}) async-start(bf16[16,16,3072]{2,1,0:T(8,128)(2,1)} %bitcast.8), calls=%async_computation.1 | async-start | bytes 3145728 | tf_op jit(solution)/shard_map/all_to_all | solution.py:204
  65.4 0.0 copy-done.6
  65.4 0.0 copy-done.5
  65.4 0.2 shard_map.104.weight_ref
  65.6 53.4 %all-to-all-done.1 = bf16[16,16,3072]{2,1,0:T(8,128)(2,1)S(1)} async-done(((bf16[16,16,3072]{2,1,0:T(8,128)(2,1)}), bf16[16,16,3072]{2,1,0:T(8,128)(2,1)S(1)}, u32[]{:S(2)}, u32[]{:S(2)}) %all-to-all-start.1) | async-done | bytes 1572896 | tf_op jit(solution)/shard_map/all_to_all | solution.py:204
  119.1 1.2 shard_map.105
  120.2 0.0 copy-start.1
  120.3 0.0 copy-start.3
  120.3 43.5 %all_to_all.26 = bf16[16,16,2048]{2,1,0:T(8,128)(2,1)S(1)} all-to-all(bf16[16,16,2048]{2,1,0:T(8,128)(2,1)S(1)} %bitcast.33), channel_id=1, replica_groups=mesh['ep'=16,'edp'=64] {'ep'}, dimensions={0} | all-to-all | bytes 2097152 | tf_op jit(solution)/shard_map/all_to_all | solution.py:216
  163.8 7.7 %all-to-all-start.4 = ((bf16[16,16,1024]{2,1,0:T(8,128)(2,1)}), bf16[16,16,1024]{2,1,0:T(8,128)(2,1)S(1)}, u32[]{:S(2)}, u32[]{:S(2)}) async-start(bf16[16,16,1024]{2,1,0:T(8,128)(2,1)} %bitcast.19), calls=%async_computation.4 | async-start | bytes 1048576 | tf_op jit(solution)/shard_map/all_to_all | solution.py:219
  171.4 0.0 copy-done.1
  171.5 0.0 copy-done.3
  171.5 1.2 shard_map.106
  172.7 15.2 %all-to-all-done.4 = bf16[16,16,1024]{2,1,0:T(8,128)(2,1)S(1)} async-done(((bf16[16,16,1024]{2,1,0:T(8,128)(2,1)}), bf16[16,16,1024]{2,1,0:T(8,128)(2,1)S(1)}, u32[]{:S(2)}, u32[]{:S(2)}) %all-to-all-start.4) | async-done | bytes 524320 | tf_op jit(solution)/shard_map/all_to_all | solution.py:219
  187.9 4.8 %all-to-all-start.3 = ((bf16[64,8,128]{2,1,0:T(8,128)(2,1)}), bf16[64,8,128]{2,1,0:T(8,128)(2,1)S(1)}, u32[]{:S(2)}, u32[]{:S(2)}) async-start(bf16[64,8,128]{2,1,0:T(8,128)(2,1)} %bitcast.14), calls=%async_computation.3 | async-start | bytes 262144 | tf_op jit(solution)/shard_map/all_to_all | solution.py:232
  192.6 1.2 shard_map.109
  193.8 8.0 %all-to-all-done.3 = bf16[64,8,128]{2,1,0:T(8,128)(2,1)S(1)} async-done(((bf16[64,8,128]{2,1,0:T(8,128)(2,1)}), bf16[64,8,128]{2,1,0:T(8,128)(2,1)S(1)}, u32[]{:S(2)}, u32[]{:S(2)}) %all-to-all-start.3) | async-done | bytes 131104 | tf_op jit(solution)/shard_map/all_to_all | solution.py:232
  201.8 0.3 shard_map.107
  202.1 7.9 %collective-permute-start.1 = (bf16[64,128]{1,0:T(8,128)(2,1)S(1)}, bf16[64,128]{1,0:T(8,128)(2,1)S(1)}, u32[]{:S(2)}, u32[]{:S(2)}) collective-permute-start(bf16[64,128]{1,0:T(8,128)(2,1)S(1)} %shard_map.107), channel_id=1, source_target_pairs={{0,0},{16,1},{32,2},{48,3},{64,4},{80,5},{96,6},{112,7},{128,8},{1... | collective-permute-start | bytes 49160 | tf_op jit(solution)/shard_map/ppermute | solution.py:250
  210.0 1.3 shard_map.108
  211.2 8.2 %collective-permute-done.1 = bf16[64,128]{1,0:T(8,128)(2,1)S(1)} collective-permute-done((bf16[64,128]{1,0:T(8,128)(2,1)S(1)}, bf16[64,128]{1,0:T(8,128)(2,1)S(1)}, u32[]{:S(2)}, u32[]{:S(2)}) %collective-permute-start.1) | collective-permute-done | bytes 16416 | tf_op jit(solution)/shard_map/ppermute | solution.py:250
  219.4 0.6 copy.12
  (2 shorter events, 0.0 us)
Async XLA Ops:
  2.2 19.9 %collective-permute-start = (bf16[144,128]{1,0:T(8,128)(2,1)S(1)}, bf16[144,128]{1,0:T(8,128)(2,1)S(1)}, u32[]{:S(2)}, u32[]{:S(2)}) collective-permute-start(bf16[144,128]{1,0:T(8,128)(2,1)S(1)} %maximum_maximum_fusion), channel_id=1, source_target_pairs={{0,0},{1,16},{2,32},{3,48},{4,64},{5,80},{6,96},{7,112},{8,128},{9... | collective-permute-start | bytes 110600 | tf_op jit(solution)/shard_map/ppermute | solution.py:175
  48.1 1.0 copy-start
  49.1 1.0 copy-start.2
  50.2 1.0 copy-start.4
  53.0 12.4 %copy-start.6 = (s32[128,8]{0,1:T(8,128)S(1)}, s32[128,8]{0,1:T(8,128)}, u32[]{:S(2)}) copy-start(s32[128,8]{0,1:T(8,128)} %param.10) | copy-start | bytes 12292
  53.0 12.4 %copy-start.5 = (f32[128,8]{0,1:T(8,128)S(1)}, f32[128,8]{0,1:T(8,128)}, u32[]{:S(2)}) copy-start(f32[128,8]{0,1:T(8,128)} %param.9) | copy-start | bytes 12292
  53.0 66.0 %all-to-all-start.1 = ((bf16[16,16,3072]{2,1,0:T(8,128)(2,1)}), bf16[16,16,3072]{2,1,0:T(8,128)(2,1)S(1)}, u32[]{:S(2)}, u32[]{:S(2)}) async-start(bf16[16,16,3072]{2,1,0:T(8,128)(2,1)} %bitcast.8), calls=%async_computation.1 | async-start | bytes 3145728 | tf_op jit(solution)/shard_map/all_to_all | solution.py:204
  120.2 51.2 %copy-start.1 = (bf16[1,256,1024]{2,1,0:T(8,128)(2,1)S(1)}, bf16[1,256,1024]{2,1,0:T(8,128)(2,1)}, u32[]{:S(2)}) copy-start(bf16[1,256,1024]{2,1,0:T(8,128)(2,1)} %param.11) | copy-start | bytes 1572868
  120.3 51.2 %copy-start.3 = (bf16[1,256,1024]{2,1,0:T(8,128)(2,1)S(1)}, bf16[1,256,1024]{2,1,0:T(8,128)(2,1)}, u32[]{:S(2)}) copy-start(bf16[1,256,1024]{2,1,0:T(8,128)(2,1)} %param.12) | copy-start | bytes 1572868
  163.8 24.1 %all-to-all-start.4 = ((bf16[16,16,1024]{2,1,0:T(8,128)(2,1)}), bf16[16,16,1024]{2,1,0:T(8,128)(2,1)S(1)}, u32[]{:S(2)}, u32[]{:S(2)}) async-start(bf16[16,16,1024]{2,1,0:T(8,128)(2,1)} %bitcast.19), calls=%async_computation.4 | async-start | bytes 1048576 | tf_op jit(solution)/shard_map/all_to_all | solution.py:219
  187.9 13.9 %all-to-all-start.3 = ((bf16[64,8,128]{2,1,0:T(8,128)(2,1)}), bf16[64,8,128]{2,1,0:T(8,128)(2,1)S(1)}, u32[]{:S(2)}, u32[]{:S(2)}) async-start(bf16[64,8,128]{2,1,0:T(8,128)(2,1)} %bitcast.14), calls=%async_computation.3 | async-start | bytes 262144 | tf_op jit(solution)/shard_map/all_to_all | solution.py:232
  202.1 17.4 %collective-permute-start.1 = (bf16[64,128]{1,0:T(8,128)(2,1)S(1)}, bf16[64,128]{1,0:T(8,128)(2,1)S(1)}, u32[]{:S(2)}, u32[]{:S(2)}) collective-permute-start(bf16[64,128]{1,0:T(8,128)(2,1)S(1)} %shard_map.107), channel_id=1, source_target_pairs={{0,0},{16,1},{32,2},{48,3},{64,4},{80,5},{96,6},{112,7},{128,8},{1... | collective-permute-start | bytes 49160 | tf_op jit(solution)/shard_map/ppermute | solution.py:250

commit v2 on v1

--- a/solution.py
+++ b/solution.py
@@ -65,7 +65,17 @@
     out_ref[...] = jnp.broadcast_to(jnp.sum(picked, axis=1, keepdims=True), (CAP, toks))
 
 
-def project_body(recv_ref, gate_ref, up_ref, down_ref, part_ref, x_ref, y_ref):
+def project_body(
+    recv_ref, gate_hbm, up_hbm, down_hbm, part_ref, x_ref, y_ref, gate_ref, up_ref, down_ref, sems
+):
+    loads = [
+        pltpu.make_async_copy(src, dst, sems.at[k])
+        for k, (src, dst) in enumerate(
+            ((gate_hbm, gate_ref), (up_hbm, up_ref), (down_hbm, down_ref))
+        )
+    ]
+    for load in loads:
+        load.start()
     rows = recv_ref.shape[0] // 4
     for q in range(4):
         block = recv_ref[q * rows : (q + 1) * rows, :]
@@ -74,14 +84,17 @@
     x = x_ref[...]
     y = y_ref[...]
     hid = gate_ref.shape[1]
+    loads[0].wait()
     part_ref[:, 0:hid] = jnp.dot(x, gate_ref[...], preferred_element_type=F32).astype(BF16)
+    loads[1].wait()
     part_ref[:, hid : 2 * hid] = jnp.dot(x, up_ref[...], preferred_element_type=F32).astype(BF16)
+    loads[2].wait()
     part_ref[:, 2 * hid : 3 * hid] = lax.dot_general(
         y, down_ref[...], LAST, preferred_element_type=F32
     ).astype(BF16)
 
 
-def hidden_body(parts_ref, weight_ref, grads_ref, weighted_ref):
+def hidden_body(parts_ref, weight_ref, grads_ref):
     peers = parts_ref.shape[0] // CAP
     hid = parts_ref.shape[1] // 3
     total = parts_ref[0:CAP, :].astype(F32)
@@ -101,7 +114,7 @@
         rows = slice(s * CAP, (s + 1) * CAP)
         grads_ref[rows, 0:hid] = gate_grad
         grads_ref[rows, hid : 2 * hid] = up_grad
-        weighted_ref[rows, :] = hidden_weighted
+        grads_ref[rows, 2 * hid : 3 * hid] = hidden_weighted
 
 
 def slot_grad_body(grads_ref, gate_ref, up_ref, out_ref):
@@ -122,7 +135,7 @@
         ).astype(BF16)
 
 
-def weight_grads_body(x_ref, grads_ref, gate_ref, up_ref):
+def weight_grads_body(x_ref, y_ref, grads_ref, gate_ref, up_ref, down_ref):
     hid = gate_ref.shape[1]
     x = x_ref[...]
     gate_ref[...] = lax.dot_general(
@@ -131,11 +144,8 @@
     up_ref[...] = lax.dot_general(
         x, grads_ref[:, hid : 2 * hid], FIRST, preferred_element_type=F32
     ).astype(BF16)
-
-
-def down_grad_body(weighted_ref, y_ref, out_ref):
-    out_ref[...] = lax.dot_general(
-        weighted_ref[...], y_ref[...], FIRST, preferred_element_type=F32
+    down_ref[...] = lax.dot_general(
+        grads_ref[:, 2 * hid : 3 * hid], y_ref[...], FIRST, preferred_element_type=F32
     ).astype(BF16)
 
 
@@ -177,6 +187,8 @@
     mine = (ids == lax.axis_index("edp")).astype(F32)
     weight = call(weight_body, arr((CAP, toks), F32), 10**5, 10**4, mine, probs.T)
 
+    packed, weight = lax.optimization_barrier((packed, weight))
+
     def body(*refs):
         dispatch_body(experts, *refs)
 
@@ -191,34 +203,30 @@
         sent.reshape(experts, CAP, 2 * width), "edp", split_axis=0, concat_axis=0, tiled=True
     ).reshape(experts * CAP, 2 * width)
 
-    part, x_s, y_s = call(
+    part, x_s, y_s = pl.pallas_call(
         project_body,
-        (arr((slots, 3 * hid)), arr((slots, wide)), arr((slots, wide))),
-        6 * slots * wide * hid,
-        4 * 10**6,
-        recv,
-        gate,
-        up,
-        down,
-    )
+        out_shape=(arr((slots, 3 * hid)), arr((slots, wide)), arr((slots, wide))),
+        in_specs=[pl.BlockSpec(memory_space=pltpu.VMEM)]
+        + [pl.BlockSpec(memory_space=pl.ANY)] * 3,
+        scratch_shapes=[
+            pltpu.VMEM((wide, hid), BF16),
+            pltpu.VMEM((wide, hid), BF16),
+            pltpu.VMEM((hid, wide), BF16),
+            pltpu.SemaphoreType.DMA((3,)),
+        ],
+        compiler_params=pltpu.CompilerParams(vmem_limit_bytes=40 * 1024 * 1024),
+        cost_estimate=pl.CostEstimate(
+            flops=6 * slots * wide * hid, bytes_accessed=4 * 10**6, transcendentals=0
+        ),
+    )(recv, gate, up, down)
     parts = lax.all_to_all(
         part.reshape(blocks, CAP, 3 * hid), "ep", split_axis=0, concat_axis=0, tiled=True
     ).reshape(slots, 3 * hid)
 
-    grads, weighted = call(
-        hidden_body,
-        (arr((slots, 2 * hid)), arr((slots, hid))),
-        10**6,
-        3 * 10**6,
-        parts,
-        weight,
-    )
+    grads = call(hidden_body, arr((slots, 3 * hid)), 10**6, 3 * 10**6, parts, weight)
     grads = lax.all_to_all(
-        grads.reshape(blocks, CAP, 2 * hid), "ep", split_axis=0, concat_axis=0, tiled=True
-    ).reshape(slots, 2 * hid)
-    weighted = lax.all_to_all(
-        weighted.reshape(blocks, CAP, hid), "ep", split_axis=0, concat_axis=0, tiled=True
-    ).reshape(slots, hid)
+        grads.reshape(blocks, CAP, 3 * hid), "ep", split_axis=0, concat_axis=0, tiled=True
+    ).reshape(slots, 3 * hid)
 
     slot_grad = call(
         slot_grad_body,
@@ -233,19 +241,18 @@
         slot_grad.reshape(experts, 8, 128), "edp", split_axis=0, concat_axis=0, tiled=True
     ).reshape(experts * 8, 128)
 
-    grad_gate, grad_up = call(
-        weight_grads_body,
-        (arr((wide, hid)), arr((wide, hid))),
-        4 * slots * wide * hid,
-        2 * 10**6,
-        x_s,
-        grads,
-    )
-    grad_down = call(
-        down_grad_body, arr((hid, wide)), 2 * slots * wide * hid, 10**6, weighted, y_s
-    )
     token_grad = call(
         combine_body, arr((width, toks)), 4 * experts * 8 * 128 * toks, 4 * 10**5, returned, disp
+    )
+    grads, token_grad = lax.optimization_barrier((grads, token_grad))
+    grad_gate, grad_up, grad_down = call(
+        weight_grads_body,
+        (arr((wide, hid)), arr((wide, hid)), arr((hid, wide))),
+        6 * slots * wide * hid,
+        4 * 10**6,
+        x_s,
+        y_s,
+        grads,
     )
     token_grad = lax.ppermute(token_grad, ("ep", "edp"), back).T
     return (token_grad, grad_gate[None], grad_up[None], grad_down[None])

time: 221 us -> 191 us (0.86)
  the two profiles are of different devices: /device:TPU:44 before, /device:TPU:42 now
where the time goes in v2:
time: 191 us
  blocking collectives  145 us (76%)
  starting transfers between devices  22.5 us (12%)
  waiting for transfers between devices  11.5 us (6%)
  Pallas kernels  4.58 us (2%)
  local copies, waits for them, and re-layouts  4.51 us (2%)
  other arithmetic  2.2 us (1%)
    all_to_all x1, blocking collectives, per_device(): lax.all_to_all(part.reshape(blocks, CAP, 3 * hid), 'ep', split_axis=0, co...  56.9 us
    all_to_all x1, blocking collectives, per_device(): lax.all_to_all(grads.reshape(blocks, CAP, 3 * hid), 'ep', split_axis=0, c...  49.4 us
    all_to_all x1, blocking collectives, per_device(): lax.all_to_all(sent.reshape(experts, CAP, 2 * width), 'edp', split_axis=0...  23.3 us
    ppermute x1, starting transfers between devices, per_device(): packed = lax.ppermute(packed, ('ep', 'edp'), there)  18.1 us
    all_to_all x1, blocking collectives, per_device(): lax.all_to_all(slot_grad.reshape(experts, 8, 128), 'edp', split_axis=0, c...  15.3 us
    ppermute x1, waiting for transfers between devices, per_device(): token_grad = lax.ppermute(token_grad, ('ep', 'edp'), back).T  11.5 us
    unnamed x13, local copies, waits for them, and re-layouts  4.43 us
    ppermute x1, starting transfers between devices, per_device(): token_grad = lax.ppermute(token_grad, ('ep', 'edp'), back).T  4.41 us
  transfers between devices with their start and end apart: 2, of which 1 were waited for; matrix products, arithmetic and copies ran while one was open for 0% of the time, Pallas kernels for 1%

profile of v2, /device:TPU:42, one launch (start us, length us, event | category | flops | bytes accessed | tf_op | source)
XLA Modules:
  0.0 190.9 jit_solution(6558299198455369872)
XLA Ops:
  0.6 0.7 convert_bitcast_fusion.1
  1.3 0.1 pad.3.clone
  1.4 0.8 maximum_maximum_fusion
  2.2 18.1 %collective-permute-start = (bf16[144,128]{1,0:T(8,128)(2,1)S(1)}, bf16[144,128]{1,0:T(8,128)(2,1)S(1)}, u32[]{:S(2)}, u32[]{:S(2)}) collective-permute-start(bf16[144,128]{1,0:T(8,128)(2,1)S(1)} %maximum_maximum_fusion), channel_id=1, source_target_pairs={{0,0},{1,16},{2,32},{3,48},{4,64},{5,80},{6,96},{7,112},{8,128},{9... | collective-permute-start | bytes 110600 | tf_op jit(solution)/shard_map/ppermute | solution.py:185
  20.3 0.7 convert_bitcast_fusion.mine_ref
  21.0 0.0 copy-start.5
  21.0 0.7 copy-done.5
  21.7 0.2 shard_map.102.weight_ref
  21.9 0.0 collective-permute-done.refs_0_
  22.0 0.4 shard_map.103
  22.3 23.3 %all_to_all.20 = bf16[64,16,128]{2,1,0:T(8,128)(2,1)S(1)} all-to-all(bf16[64,16,128]{2,1,0:T(8,128)(2,1)S(1)} %bitcast.35), channel_id=1, replica_groups=mesh['ep'=16,'edp'=64] {'edp'}, dimensions={0} | all-to-all | bytes 524288 | tf_op jit(solution)/shard_map/all_to_all | solution.py:202
  45.6 0.0 copy-start
  45.6 1.0 copy-done
  46.6 0.0 copy-start.2
  46.6 1.0 copy-done.2
  47.7 0.0 copy-start.4
  47.7 1.0 copy-done.4
  48.7 1.3 shard_map.104
  50.0 56.9 %all_to_all.21 = bf16[16,16,3072]{2,1,0:T(8,128)(2,1)S(1)} all-to-all(bf16[16,16,3072]{2,1,0:T(8,128)(2,1)S(1)} %bitcast.30), channel_id=1, replica_groups=mesh['ep'=16,'edp'=64] {'ep'}, dimensions={0} | all-to-all | bytes 3145728 | tf_op jit(solution)/shard_map/all_to_all | solution.py:222
  106.9 0.4 shard_map.105
  107.4 0.0 copy-start.1
  107.4 0.0 copy-start.3
  107.4 49.4 %all_to_all.22 = bf16[16,16,3072]{2,1,0:T(8,128)(2,1)S(1)} all-to-all(bf16[16,16,3072]{2,1,0:T(8,128)(2,1)S(1)} %bitcast.25), channel_id=1, replica_groups=mesh['ep'=16,'edp'=64] {'ep'}, dimensions={0} | all-to-all | bytes 3145728 | tf_op jit(solution)/shard_map/all_to_all | solution.py:227
  156.8 0.0 copy-done.1
  156.8 0.0 copy-done.3
  156.8 0.5 shard_map.106
  157.3 15.3 %all_to_all.23 = bf16[64,8,128]{2,1,0:T(8,128)(2,1)S(1)} all-to-all(bf16[64,8,128]{2,1,0:T(8,128)(2,1)S(1)} %bitcast.34), channel_id=1, replica_groups=mesh['ep'=16,'edp'=64] {'edp'}, dimensions={0} | all-to-all | bytes 262144 | tf_op jit(solution)/shard_map/all_to_all | solution.py:240
  172.7 0.3 shard_map.107
  172.9 4.4 %collective-permute-start.1 = (bf16[64,128]{1,0:T(8,128)(2,1)S(1)}, bf16[64,128]{1,0:T(8,128)(2,1)S(1)}, u32[]{:S(2)}, u32[]{:S(2)}) collective-permute-start(bf16[64,128]{1,0:T(8,128)(2,1)S(1)} %shard_map.107), channel_id=1, source_target_pairs={{0,0},{16,1},{32,2},{48,3},{64,4},{80,5},{96,6},{112,7},{128,8},{1... | collective-permute-start | bytes 49160 | tf_op jit(solution)/shard_map/ppermute | solution.py:257
  177.4 1.5 shard_map.108
  178.8 11.5 %collective-permute-done.1 = bf16[64,128]{1,0:T(8,128)(2,1)S(1)} collective-permute-done((bf16[64,128]{1,0:T(8,128)(2,1)S(1)}, bf16[64,128]{1,0:T(8,128)(2,1)S(1)}, u32[]{:S(2)}, u32[]{:S(2)}) %collective-permute-start.1) | collective-permute-done | bytes 16416 | tf_op jit(solution)/shard_map/ppermute | solution.py:257
  190.3 0.6 copy.12
  (1 shorter events, 0.0 us)
Async XLA Ops:
  2.2 19.7 %collective-permute-start = (bf16[144,128]{1,0:T(8,128)(2,1)S(1)}, bf16[144,128]{1,0:T(8,128)(2,1)S(1)}, u32[]{:S(2)}, u32[]{:S(2)}) collective-permute-start(bf16[144,128]{1,0:T(8,128)(2,1)S(1)} %maximum_maximum_fusion), channel_id=1, source_target_pairs={{0,0},{1,16},{2,32},{3,48},{4,64},{5,80},{6,96},{7,112},{8,128},{9... | collective-permute-start | bytes 110600 | tf_op jit(solution)/shard_map/ppermute | solution.py:185
  21.0 0.7 copy-start.5
  45.6 1.0 copy-start
  46.6 1.0 copy-start.2
  47.7 1.0 copy-start.4
  107.4 49.4 %copy-start.1 = (bf16[1,256,1024]{2,1,0:T(8,128)(2,1)S(1)}, bf16[1,256,1024]{2,1,0:T(8,128)(2,1)}, u32[]{:S(2)}) copy-start(bf16[1,256,1024]{2,1,0:T(8,128)(2,1)} %param.11) | copy-start | bytes 1572868
  107.4 49.4 %copy-start.3 = (bf16[1,256,1024]{2,1,0:T(8,128)(2,1)S(1)}, bf16[1,256,1024]{2,1,0:T(8,128)(2,1)}, u32[]{:S(2)}) copy-start(bf16[1,256,1024]{2,1,0:T(8,128)(2,1)} %param.12) | copy-start | bytes 1572868
  172.9 17.4 %collective-permute-start.1 = (bf16[64,128]{1,0:T(8,128)(2,1)S(1)}, bf16[64,128]{1,0:T(8,128)(2,1)S(1)}, u32[]{:S(2)}, u32[]{:S(2)}) collective-permute-start(bf16[64,128]{1,0:T(8,128)(2,1)S(1)} %shard_map.107), channel_id=1, source_target_pairs={{0,0},{16,1},{32,2},{48,3},{64,4},{80,5},{96,6},{112,7},{128,8},{1... | collective-permute-start | bytes 49160 | tf_op jit(solution)/shard_map/ppermute | solution.py:257

commit v3 on v2

--- a/solution.py
+++ b/solution.py
@@ -51,7 +51,7 @@
     ).astype(BF16)
 
 
-def weight_body(mine_ref, probs_ref, out_ref):
+def weight_body(mine_ref, probs_ref, gate_ref, up_ref, down_ref, out_ref):
     mine = mine_ref[...]
     toks = mine.shape[1]
     mask = jnp.sum(mine, axis=0, keepdims=True)
@@ -77,8 +77,9 @@
     for load in loads:
         load.start()
     rows = recv_ref.shape[0] // 4
+    recv = recv_ref[...].reshape(rows // CAP, 4, CAP, 128)
     for q in range(4):
-        block = recv_ref[q * rows : (q + 1) * rows, :]
+        block = recv[:, q].reshape(rows, 128)
         x_ref[:, q * 64 : (q + 1) * 64] = block[:, :64]
         y_ref[:, q * 64 : (q + 1) * 64] = block[:, 64:]
     x = x_ref[...]
@@ -124,15 +125,16 @@
     ) + lax.dot_general(
         grads_ref[:, hid : 2 * hid], up_ref[...], LAST, preferred_element_type=F32
     )
-    rows = slot_grad.shape[0]
-    pairs = slot_grad.reshape(rows // 16, 2, 8, slot_grad.shape[1])
-    low = pairs[:, 0].reshape(rows // 2, slot_grad.shape[1])
-    high = pairs[:, 1].reshape(rows // 2, slot_grad.shape[1])
+    blocks = slot_grad.shape[0] // CAP
+    wide = slot_grad.shape[1]
+    pairs = slot_grad.reshape(blocks, 2, 8, wide)
+    low, high = pairs[:, 0], pairs[:, 1]
+    shares = []
     for q in range(4):
         cols = slice(q * 64, (q + 1) * 64)
-        out_ref[q * (rows // 2) : (q + 1) * (rows // 2), :] = jnp.concatenate(
-            [low[:, cols], high[:, cols]], axis=1
-        ).astype(BF16)
+        shares.append(jnp.concatenate([low[:, :, cols], high[:, :, cols]], axis=2)[:, None])
+    out = jnp.concatenate(shares, axis=1).reshape(4 * 8 * blocks, 128)
+    out_ref[...] = out.astype(BF16)
 
 
 def weight_grads_body(x_ref, y_ref, grads_ref, gate_ref, up_ref, down_ref):
@@ -172,7 +174,7 @@
     gate, up, down = w_gate[0], w_up[0], w_down[0]
 
     there = [
-        (b * experts + j, (j // share) * experts + (j % share) * blocks + b)
+        (b * experts + j, (j // share) * experts + b * share + j % share)
         for b in range(blocks)
         for j in range(experts)
     ]
@@ -185,7 +187,13 @@
     packed = lax.ppermute(packed, ("ep", "edp"), there)
 
     mine = (ids == lax.axis_index("edp")).astype(F32)
-    weight = call(weight_body, arr((CAP, toks), F32), 10**5, 10**4, mine, probs.T)
+    weight = pl.pallas_call(
+        weight_body,
+        out_shape=arr((CAP, toks), F32),
+        in_specs=[pl.BlockSpec(memory_space=pltpu.VMEM)] * 2
+        + [pl.BlockSpec(memory_space=pl.ANY)] * 3,
+        cost_estimate=pl.CostEstimate(flops=10**5, bytes_accessed=10**4, transcendentals=0),
+    )(mine, probs.T, gate, up, down)
 
     packed, weight = lax.optimization_barrier((packed, weight))
 

time: 191 us -> 189 us (0.990)
  the two profiles are of different devices: /device:TPU:42 before, /device:TPU:10 now
where the time goes in v3:
time: 189 us; the launch traced here: 188 us
  blocking collectives  151 us (80%)
  starting transfers between devices  19.1 us (10%)
  waiting for transfers between devices  8.21 us (4%)
  Pallas kernels  5.89 us (3%)
  other arithmetic  2.9 us (2%)
    all_to_all x1, blocking collectives, per_device(): lax.all_to_all(part.reshape(blocks, CAP, 3 * hid), 'ep', split_axis=0, co...  56.3 us
    all_to_all x1, blocking collectives, per_device(): lax.all_to_all(grads.reshape(blocks, CAP, 3 * hid), 'ep', split_axis=0, c...  49 us
    all_to_all x1, blocking collectives, per_device(): lax.all_to_all(sent.reshape(experts, CAP, 2 * width), 'edp', split_axis=0...  30.1 us
    all_to_all x1, blocking collectives, per_device(): lax.all_to_all(slot_grad.reshape(experts, 8, 128), 'edp', split_axis=0, c...  15.5 us
    ppermute x1, starting transfers between devices, per_device(): packed = lax.ppermute(packed, ('ep', 'edp'), there)  13.5 us
    ppermute x1, waiting for transfers between devices, per_device(): token_grad = lax.ppermute(token_grad, ('ep', 'edp'), back).T  8.2 us
    ppermute x1, starting transfers between devices, per_device(): token_grad = lax.ppermute(token_grad, ('ep', 'edp'), back).T  5.57 us
  transfers between devices with their start and end apart: 2, of which 1 were waited for; matrix products, arithmetic and copies ran while one was open for 1% of the time, Pallas kernels for 2%

profile of v3, /device:TPU:10, one launch (start us, length us, event | category | flops | bytes accessed | tf_op | source)
XLA Modules:
  0.0 188.3 jit_solution(5394298197448481742)
XLA Ops:
  0.6 0.0 copy-start.2
  0.6 0.0 copy-start.1
  0.7 0.0 copy-start
  0.7 0.8 convert_bitcast_fusion.1
  1.5 0.1 pad.3.clone
  1.6 0.8 maximum_maximum_fusion
  2.4 13.5 %collective-permute-start = (bf16[144,128]{1,0:T(8,128)(2,1)S(1)}, bf16[144,128]{1,0:T(8,128)(2,1)S(1)}, u32[]{:S(2)}, u32[]{:S(2)}) collective-permute-start(bf16[144,128]{1,0:T(8,128)(2,1)S(1)} %maximum_maximum_fusion), channel_id=1, source_target_pairs={{0,0},{1,1},{2,2},{3,3},{4,64},{5,65},{6,66},{7,67},{8,128},{9,129... | collective-permute-start | bytes 110600 | tf_op jit(solution)/shard_map/ppermute | solution.py:187
  15.9 1.3 convert_bitcast_fusion.mine_ref
  17.2 1.5 shard_map.102.weight_ref
  18.7 0.0 collective-permute-done.refs_0_
  18.7 0.4 shard_map.103
  19.1 30.1 %all_to_all.20 = bf16[64,16,128]{2,1,0:T(8,128)(2,1)S(1)} all-to-all(bf16[64,16,128]{2,1,0:T(8,128)(2,1)S(1)} %bitcast.38), channel_id=1, replica_groups=mesh['ep'=16,'edp'=64] {'edp'}, dimensions={0} | all-to-all | bytes 524288 | tf_op jit(solution)/shard_map/all_to_all | solution.py:210
  49.2 0.0 copy-done.2
  49.2 0.0 copy-done.1
  49.2 0.0 copy-done
  49.2 1.3 shard_map.104
  50.5 0.0 copy-start.3
  50.5 56.3 %all_to_all.21 = bf16[16,16,3072]{2,1,0:T(8,128)(2,1)S(1)} all-to-all(bf16[16,16,3072]{2,1,0:T(8,128)(2,1)S(1)} %bitcast.34), channel_id=1, replica_groups=mesh['ep'=16,'edp'=64] {'ep'}, dimensions={0} | all-to-all | bytes 3145728 | tf_op jit(solution)/shard_map/all_to_all | solution.py:230
  106.8 0.0 copy-done.3
  106.8 0.4 shard_map.105
  107.2 49.0 %all_to_all.22 = bf16[16,16,3072]{2,1,0:T(8,128)(2,1)S(1)} all-to-all(bf16[16,16,3072]{2,1,0:T(8,128)(2,1)S(1)} %bitcast.25), channel_id=1, replica_groups=mesh['ep'=16,'edp'=64] {'ep'}, dimensions={0} | all-to-all | bytes 3145728 | tf_op jit(solution)/shard_map/all_to_all | solution.py:235
  156.2 0.5 shard_map.106
  156.7 15.5 %all_to_all.23 = bf16[64,8,128]{2,1,0:T(8,128)(2,1)S(1)} all-to-all(bf16[64,8,128]{2,1,0:T(8,128)(2,1)S(1)} %bitcast.37), channel_id=1, replica_groups=mesh['ep'=16,'edp'=64] {'edp'}, dimensions={0} | all-to-all | bytes 262144 | tf_op jit(solution)/shard_map/all_to_all | solution.py:248
  172.2 0.3 shard_map.107
  172.5 5.6 %collective-permute-start.1 = (bf16[64,128]{1,0:T(8,128)(2,1)S(1)}, bf16[64,128]{1,0:T(8,128)(2,1)S(1)}, u32[]{:S(2)}, u32[]{:S(2)}) collective-permute-start(bf16[64,128]{1,0:T(8,128)(2,1)S(1)} %shard_map.107), channel_id=1, source_target_pairs={{0,0},{1,1},{2,2},{3,3},{64,4},{65,5},{66,6},{67,7},{128,8},{129,9... | collective-permute-start | bytes 49160 | tf_op jit(solution)/shard_map/ppermute | solution.py:265
  178.1 1.5 shard_map.108
  179.5 8.2 %collective-permute-done.1 = bf16[64,128]{1,0:T(8,128)(2,1)S(1)} collective-permute-done((bf16[64,128]{1,0:T(8,128)(2,1)S(1)}, bf16[64,128]{1,0:T(8,128)(2,1)S(1)}, u32[]{:S(2)}, u32[]{:S(2)}) %collective-permute-start.1) | collective-permute-done | bytes 16416 | tf_op jit(solution)/shard_map/ppermute | solution.py:265
  187.7 0.6 copy.12
  (1 shorter events, 0.0 us)
Async XLA Ops:
  0.6 48.5 %copy-start.2 = (bf16[1,1024,256]{2,1,0:T(8,128)(2,1)S(1)}, bf16[1,1024,256]{2,1,0:T(8,128)(2,1)}, u32[]{:S(2)}) copy-start(bf16[1,1024,256]{2,1,0:T(8,128)(2,1)} %param.13) | copy-start | bytes 1572868
  0.6 48.5 %copy-start.1 = (bf16[1,256,1024]{2,1,0:T(8,128)(2,1)S(1)}, bf16[1,256,1024]{2,1,0:T(8,128)(2,1)}, u32[]{:S(2)}) copy-start(bf16[1,256,1024]{2,1,0:T(8,128)(2,1)} %param.12) | copy-start | bytes 1572868
  0.7 48.5 %copy-start = (bf16[1,256,1024]{2,1,0:T(8,128)(2,1)S(1)}, bf16[1,256,1024]{2,1,0:T(8,128)(2,1)}, u32[]{:S(2)}) copy-start(bf16[1,256,1024]{2,1,0:T(8,128)(2,1)} %param.11) | copy-start | bytes 1572868
  2.4 16.3 %collective-permute-start = (bf16[144,128]{1,0:T(8,128)(2,1)S(1)}, bf16[144,128]{1,0:T(8,128)(2,1)S(1)}, u32[]{:S(2)}, u32[]{:S(2)}) collective-permute-start(bf16[144,128]{1,0:T(8,128)(2,1)S(1)} %maximum_maximum_fusion), channel_id=1, source_target_pairs={{0,0},{1,1},{2,2},{3,3},{4,64},{5,65},{6,66},{7,67},{8,128},{9,129... | collective-permute-start | bytes 110600 | tf_op jit(solution)/shard_map/ppermute | solution.py:187
  50.5 56.3 %copy-start.3 = (f32[16,128]{1,0:T(8,128)S(1)}, f32[16,128]{1,0:T(8,128)}, u32[]{:S(2)}) copy-start(f32[16,128]{1,0:T(8,128)} %shard_map.102.weight_ref) | copy-start | bytes 24580
  172.5 15.2 %collective-permute-start.1 = (bf16[64,128]{1,0:T(8,128)(2,1)S(1)}, bf16[64,128]{1,0:T(8,128)(2,1)S(1)}, u32[]{:S(2)}, u32[]{:S(2)}) collective-permute-start(bf16[64,128]{1,0:T(8,128)(2,1)S(1)} %shard_map.107), channel_id=1, source_target_pairs={{0,0},{1,1},{2,2},{3,3},{64,4},{65,5},{66,6},{67,7},{128,8},{129,9... | collective-permute-start | bytes 49160 | tf_op jit(solution)/shard_map/ppermute | solution.py:265

commit v4 on v3

--- a/solution.py
+++ b/solution.py
@@ -111,15 +111,23 @@
     hidden_weighted = (weight * silu * up).astype(BF16)
     up_grad = (hidden_grad * silu).astype(BF16)
     gate_grad = (hidden_grad * up * sig * (1.0 + gate * (1.0 - sig))).astype(BF16)
-    for s in range(peers):
-        rows = slice(s * CAP, (s + 1) * CAP)
-        grads_ref[rows, 0:hid] = gate_grad
-        grads_ref[rows, hid : 2 * hid] = up_grad
-        grads_ref[rows, 2 * hid : 3 * hid] = hidden_weighted
-
-
-def slot_grad_body(grads_ref, gate_ref, up_ref, out_ref):
+    grads_ref[:, 0:hid] = gate_grad
+    grads_ref[:, hid : 2 * hid] = up_grad
+    grads_ref[:, 2 * hid : 3 * hid] = hidden_weighted
+
+
+def slot_grad_body(steps, place_ref, *refs):
+    pieces, (gate_ref, up_ref, out_ref, grads_ref) = refs[:-4], refs[-4:]
     hid = gate_ref.shape[1]
+    ring = len(steps)
+    spot = lax.div(place_ref[0], 4)
+    side = lax.rem(lax.div(place_ref[0], 2), 2)
+    way = 1 - 2 * lax.rem(place_ref[0], 2)
+    for step, piece_ref in zip(steps, pieces, strict=True):
+        pair = 2 * CAP * lax.rem(spot + step * way + ring, ring)
+        for half, z in ((0, side), (1, 1 - side)):
+            row = pl.multiple_of(pair + CAP * z, CAP)
+            grads_ref[pl.ds(row, CAP), :] = piece_ref[half * CAP : (half + 1) * CAP, :]
     slot_grad = lax.dot_general(
         grads_ref[:, 0:hid], gate_ref[...], LAST, preferred_element_type=F32
     ) + lax.dot_general(
@@ -231,20 +239,47 @@
         part.reshape(blocks, CAP, 3 * hid), "ep", split_axis=0, concat_axis=0, tiled=True
     ).reshape(slots, 3 * hid)
 
-    grads = call(hidden_body, arr((slots, 3 * hid)), 10**6, 3 * 10**6, parts, weight)
-    grads = lax.all_to_all(
-        grads.reshape(blocks, CAP, 3 * hid), "ep", split_axis=0, concat_axis=0, tiled=True
-    ).reshape(slots, 3 * hid)
-
-    slot_grad = call(
-        slot_grad_body,
-        arr((4 * slots // 2, 128)),
-        4 * slots * wide * hid,
-        2 * 10**6,
-        grads,
-        gate,
-        up,
-    )
+    mine = call(hidden_body, arr((CAP, 3 * hid)), 10**6, 2 * 10**6, parts, weight)
+
+    ring = blocks // 2
+
+    def shifted(step):
+        return [
+            (
+                b * experts + e,
+                ((b // 2 + (step if e % 2 == 0 else -step)) % ring * 2 + b % 2) * experts + e,
+            )
+            for b in range(blocks)
+            for e in range(experts)
+        ]
+
+    other = lax.ppermute(mine, "ep", [(b, b ^ 1) for b in range(blocks)])
+    right = left = jnp.concatenate([mine, other], axis=0)
+    steps, pieces = [0], [right]
+    for k in range(1, ring // 2 + 1):
+        right = lax.ppermute(right, ("ep", "edp"), shifted(1))
+        steps.append(-k)
+        pieces.append(right)
+        if k < ring - k:
+            left = lax.ppermute(left, ("ep", "edp"), shifted(-1))
+            steps.append(k)
+            pieces.append(left)
+
+    def slot_body(*refs):
+        slot_grad_body(steps, *refs)
+
+    code = lax.axis_index("ep") * 2 + lax.rem(lax.axis_index("edp"), 2)
+    rank = jnp.full((1,), code, jnp.int32)
+    slot_grad, grads = pl.pallas_call(
+        slot_body,
+        out_shape=(arr((4 * slots // 2, 128)), arr((slots, 3 * hid))),
+        in_specs=[pl.BlockSpec(memory_space=pltpu.SMEM)]
+        + [pl.BlockSpec(memory_space=pltpu.VMEM)] * (ring + 2),
+        compiler_params=pltpu.CompilerParams(vmem_limit_bytes=40 * 1024 * 1024),
+        cost_estimate=pl.CostEstimate(
+            flops=4 * slots * wide * hid, bytes_accessed=5 * 10**6, transcendentals=0
+        ),
+    )(rank, *pieces, gate, up)
     returned = lax.all_to_all(
         slot_grad.reshape(experts, 8, 128), "edp", split_axis=0, concat_axis=0, tiled=True
     ).reshape(experts * 8, 128)

time: 189 us -> 189 us (level)
  blocking collectives: 151 us -> 105 us
  starting transfers between devices: 19.1 us -> 43.6 us
  waiting for transfers between devices: 8.21 us -> 29.7 us
    all_to_all x1 -> x0, blocking collectives: 49 us -> none  [per_device(): lax.all_to_all(grads.reshape(blocks, CAP, 3 * hid), 'ep', split_axis=0, c...]
    ppermute x0 -> x8, starting transfers between devices: none -> 24.2 us  [the longest x3 12.2 us: per_device(): left = lax.ppermute(left, ('ep', 'edp'), shifted(-1))]
    ppermute x0 -> x8, waiting for transfers between devices: none -> 21.9 us  [the longest x4 13.7 us: per_device(): right = lax.ppermute(right, ('ep', 'edp'), shifted(1))]
    all_to_all x1, blocking collectives: 15.5 us -> 18.4 us  [per_device(): lax.all_to_all(slot_grad.reshape(experts, 8, 128), 'edp', split_axis=0, c...]
  transfers between devices with their start and end apart: 2 -> 10, of which waited for: 1 -> 6; matrix products, arithmetic and copies ran while one was open for 1% -> 1% of each run, Pallas kernels for 2% -> 2%
where the time goes in v4:
time: 189 us; the launch traced here: 188 us
  blocking collectives  105 us (56%)
  starting transfers between devices  43.6 us (23%)
  waiting for transfers between devices  29.7 us (16%)
  Pallas kernels  5.86 us (3%)
  other arithmetic  2.92 us (2%)
    all_to_all x1, blocking collectives, per_device(): lax.all_to_all(part.reshape(blocks, CAP, 3 * hid), 'ep', split_axis=0, co...  56.3 us
    all_to_all x1, blocking collectives, per_device(): lax.all_to_all(sent.reshape(experts, CAP, 2 * width), 'edp', split_axis=0...  30.1 us
    all_to_all x1, blocking collectives, per_device(): lax.all_to_all(slot_grad.reshape(experts, 8, 128), 'edp', split_axis=0, c...  18.4 us
    ppermute x4, waiting for transfers between devices, per_device(): right = lax.ppermute(right, ('ep', 'edp'), shifted(1))  13.7 us
    ppermute x1, starting transfers between devices, per_device(): packed = lax.ppermute(packed, ('ep', 'edp'), there)  13.5 us
    ppermute x3, starting transfers between devices, per_device(): left = lax.ppermute(left, ('ep', 'edp'), shifted(-1))  12.2 us
    ppermute x4, starting transfers between devices, per_device(): right = lax.ppermute(right, ('ep', 'edp'), shifted(1))  9.54 us
    ppermute x1, waiting for transfers between devices, per_device(): other = lax.ppermute(mine, 'ep', [(b, b ^ 1) for b in range(blocks)])  8.19 us
  transfers between devices with their start and end apart: 10, of which 6 were waited for; matrix products, arithmetic and copies ran while one was open for 1% of the time, Pallas kernels for 2%

profile of v4, /device:TPU:10, one launch (start us, length us, event | category | flops | bytes accessed | tf_op | source)
XLA Modules:
  0.0 188.5 jit_solution(5020533507727671008)
XLA Ops:
  0.6 0.0 copy-start.2
  0.6 0.0 copy-start.1
  0.7 0.0 copy-start
  0.7 0.8 convert_bitcast_fusion.1
  1.5 0.1 pad.5.clone
  1.6 0.8 maximum_maximum_fusion
  2.4 13.5 %collective-permute-start = (bf16[144,128]{1,0:T(8,128)(2,1)S(1)}, bf16[144,128]{1,0:T(8,128)(2,1)S(1)}, u32[]{:S(2)}, u32[]{:S(2)}) collective-permute-start(bf16[144,128]{1,0:T(8,128)(2,1)S(1)} %maximum_maximum_fusion), channel_id=1, source_target_pairs={{0,0},{1,1},{2,2},{3,3},{4,64},{5,65},{6,66},{7,67},{8,128},{9,129... | collective-permute-start | bytes 110600 | tf_op jit(solution)/shard_map/ppermute | solution.py:195
  15.9 1.3 convert_bitcast_fusion.mine_ref
  17.2 1.5 shard_map.102.weight_ref
  18.7 0.0 collective-permute-done.refs_0_
  18.7 0.4 shard_map.103
  19.1 30.1 %all_to_all.15 = bf16[64,16,128]{2,1,0:T(8,128)(2,1)S(1)} all-to-all(bf16[64,16,128]{2,1,0:T(8,128)(2,1)S(1)} %bitcast.33), channel_id=1, replica_groups=mesh['ep'=16,'edp'=64] {'edp'}, dimensions={0} | all-to-all | bytes 524288 | tf_op jit(solution)/shard_map/all_to_all | solution.py:218
  49.2 0.0 copy-done.2
  49.2 0.0 copy-done.1
  49.2 0.0 copy-done
  49.2 1.3 shard_map.104
  50.5 0.0 copy-start.3
  50.5 56.3 %all_to_all.16 = bf16[16,16,3072]{2,1,0:T(8,128)(2,1)S(1)} all-to-all(bf16[16,16,3072]{2,1,0:T(8,128)(2,1)S(1)} %bitcast.30), channel_id=1, replica_groups=mesh['ep'=16,'edp'=64] {'ep'}, dimensions={0} | all-to-all | bytes 3145728 | tf_op jit(solution)/shard_map/all_to_all | solution.py:238
  106.8 0.0 copy-done.3
  106.8 0.3 shard_map.105
  107.1 2.5 %collective-permute-start.1 = (bf16[16,3072]{1,0:T(8,128)(2,1)S(1)}, bf16[16,3072]{1,0:T(8,128)(2,1)S(1)}, u32[]{:S(2)}, u32[]{:S(2)}) collective-permute-start(bf16[16,3072]{1,0:T(8,128)(2,1)S(1)} %shard_map.105), channel_id=1, source_target_pairs={{0,64},{64,0},{128,192},{192,128},{256,320},{320,256},{384,448},{4... | collective-permute-start | bytes 294920 | tf_op jit(solution)/shard_map/ppermute | solution.py:256
  109.6 8.2 %collective-permute-done.1 = bf16[16,3072]{1,0:T(8,128)(2,1)S(1)} collective-permute-done((bf16[16,3072]{1,0:T(8,128)(2,1)S(1)}, bf16[16,3072]{1,0:T(8,128)(2,1)S(1)}, u32[]{:S(2)}, u32[]{:S(2)}) %collective-permute-start.1) | collective-permute-done | bytes 98336 | tf_op jit(solution)/shard_map/ppermute | solution.py:256
  117.8 2.9 %collective-permute-start.2 = (bf16[32,3072]{1,0:T(8,128)(2,1)S(1)}, bf16[32,3072]{1,0:T(8,128)(2,1)S(1)}, u32[]{:S(2)}, u32[]{:S(2)}) collective-permute-start(bf16[32,3072]{1,0:T(8,128)(2,1)S(1)} %pad_maximum_fusion.refs_1_), channel_id=1, source_target_pairs={{0,128},{1,897},{2,130},{3,899},{4,132},{5,901},{6,134},{7,903},{8... | collective-permute-start | bytes 589832 | tf_op jit(solution)/shard_map/ppermute | solution.py:260
  120.8 4.0 %collective-permute-start.3 = (bf16[32,3072]{1,0:T(8,128)(2,1)S(1)}, bf16[32,3072]{1,0:T(8,128)(2,1)S(1)}, u32[]{:S(2)}, u32[]{:S(2)}) collective-permute-start(bf16[32,3072]{1,0:T(8,128)(2,1)S(1)} %pad_maximum_fusion.refs_1_), channel_id=1, source_target_pairs={{0,896},{1,129},{2,898},{3,131},{4,900},{5,133},{6,902},{7,135},{8... | collective-permute-start | bytes 589832 | tf_op jit(solution)/shard_map/ppermute | solution.py:264
  124.8 3.7 %collective-permute-done.2.refs_2_ = bf16[32,3072]{1,0:T(8,128)(2,1)S(1)} collective-permute-done((bf16[32,3072]{1,0:T(8,128)(2,1)S(1)}, bf16[32,3072]{1,0:T(8,128)(2,1)S(1)}, u32[]{:S(2)}, u32[]{:S(2)}) %collective-permute-start.2) | collective-permute-done | bytes 196640 | tf_op jit(solution)/shard_map/ppermute | solution.py:260
  128.5 1.9 %collective-permute-start.4 = (bf16[32,3072]{1,0:T(8,128)(2,1)S(1)}, bf16[32,3072]{1,0:T(8,128)(2,1)S(1)}, u32[]{:S(2)}, u32[]{:S(2)}) collective-permute-start(bf16[32,3072]{1,0:T(8,128)(2,1)S(1)} %collective-permute-done.2.refs_2_), channel_id=1, source_target_pairs={{0,128},{1,897},{2,130},{3,899},{4,132},{5,901},{6,134},{7,903},{8... | collective-permute-start | bytes 589832 | tf_op jit(solution)/shard_map/ppermute | solution.py:260
  130.4 0.0 collective-permute-done.3.refs_3_
  130.4 4.0 %collective-permute-start.5 = (bf16[32,3072]{1,0:T(8,128)(2,1)S(1)}, bf16[32,3072]{1,0:T(8,128)(2,1)S(1)}, u32[]{:S(2)}, u32[]{:S(2)}) collective-permute-start(bf16[32,3072]{1,0:T(8,128)(2,1)S(1)} %collective-permute-done.3.refs_3_), channel_id=1, source_target_pairs={{0,896},{1,129},{2,898},{3,131},{4,900},{5,133},{6,902},{7,135},{8... | collective-permute-start | bytes 589832 | tf_op jit(solution)/shard_map/ppermute | solution.py:264
  134.5 3.0 %collective-permute-done.4.refs_4_ = bf16[32,3072]{1,0:T(8,128)(2,1)S(1)} collective-permute-done((bf16[32,3072]{1,0:T(8,128)(2,1)S(1)}, bf16[32,3072]{1,0:T(8,128)(2,1)S(1)}, u32[]{:S(2)}, u32[]{:S(2)}) %collective-permute-start.4) | collective-permute-done | bytes 196640 | tf_op jit(solution)/shard_map/ppermute | solution.py:260
  137.4 2.2 %collective-permute-start.6 = (bf16[32,3072]{1,0:T(8,128)(2,1)S(1)}, bf16[32,3072]{1,0:T(8,128)(2,1)S(1)}, u32[]{:S(2)}, u32[]{:S(2)}) collective-permute-start(bf16[32,3072]{1,0:T(8,128)(2,1)S(1)} %collective-permute-done.4.refs_4_), channel_id=1, source_target_pairs={{0,128},{1,897},{2,130},{3,899},{4,132},{5,901},{6,134},{7,903},{8... | collective-permute-start | bytes 589832 | tf_op jit(solution)/shard_map/ppermute | solution.py:260
  139.6 0.0 collective-permute-done.5.refs_5_
  139.6 4.1 %collective-permute-start.7 = (bf16[32,3072]{1,0:T(8,128)(2,1)S(1)}, bf16[32,3072]{1,0:T(8,128)(2,1)S(1)}, u32[]{:S(2)}, u32[]{:S(2)}) collective-permute-start(bf16[32,3072]{1,0:T(8,128)(2,1)S(1)} %collective-permute-done.5.refs_5_), channel_id=1, source_target_pairs={{0,896},{1,129},{2,898},{3,131},{4,900},{5,133},{6,902},{7,135},{8... | collective-permute-start | bytes 589832 | tf_op jit(solution)/shard_map/ppermute | solution.py:264
  143.7 1.8 collective-permute-done.6.refs_6_
  145.6 2.5 %collective-permute-start.8 = (bf16[32,3072]{1,0:T(8,128)(2,1)S(1)}, bf16[32,3072]{1,0:T(8,128)(2,1)S(1)}, u32[]{:S(2)}, u32[]{:S(2)}) collective-permute-start(bf16[32,3072]{1,0:T(8,128)(2,1)S(1)} %collective-permute-done.6.refs_6_), channel_id=1, source_target_pairs={{0,128},{1,897},{2,130},{3,899},{4,132},{5,901},{6,134},{7,903},{8... | collective-permute-start | bytes 589832 | tf_op jit(solution)/shard_map/ppermute | solution.py:260
  148.1 0.0 collective-permute-done.7.refs_7_
  148.1 5.2 %collective-permute-done.8.refs_8_ = bf16[32,3072]{1,0:T(8,128)(2,1)S(1)} collective-permute-done((bf16[32,3072]{1,0:T(8,128)(2,1)S(1)}, bf16[32,3072]{1,0:T(8,128)(2,1)S(1)}, u32[]{:S(2)}, u32[]{:S(2)}) %collective-permute-start.8) | collective-permute-done | bytes 196640 | tf_op jit(solution)/shard_map/ppermute | solution.py:260
  153.3 0.6 shard_map.106
  154.0 18.4 %all_to_all.17 = bf16[64,8,128]{2,1,0:T(8,128)(2,1)S(1)} all-to-all(bf16[64,8,128]{2,1,0:T(8,128)(2,1)S(1)} %bitcast.34), channel_id=1, replica_groups=mesh['ep'=16,'edp'=64] {'edp'}, dimensions={0} | all-to-all | bytes 262144 | tf_op jit(solution)/shard_map/all_to_all | solution.py:283
  172.3 0.3 shard_map.107
  172.6 6.0 %collective-permute-start.9 = (bf16[64,128]{1,0:T(8,128)(2,1)S(1)}, bf16[64,128]{1,0:T(8,128)(2,1)S(1)}, u32[]{:S(2)}, u32[]{:S(2)}) collective-permute-start(bf16[64,128]{1,0:T(8,128)(2,1)S(1)} %shard_map.107), channel_id=1, source_target_pairs={{0,0},{1,1},{2,2},{3,3},{64,4},{65,5},{66,6},{67,7},{128,8},{129,9... | collective-permute-start | bytes 49160 | tf_op jit(solution)/shard_map/ppermute | solution.py:300
  178.6 1.5 shard_map.108
  180.1 7.8 %collective-permute-done.9 = bf16[64,128]{1,0:T(8,128)(2,1)S(1)} collective-permute-done((bf16[64,128]{1,0:T(8,128)(2,1)S(1)}, bf16[64,128]{1,0:T(8,128)(2,1)S(1)}, u32[]{:S(2)}, u32[]{:S(2)}) %collective-permute-start.9) | collective-permute-done | bytes 16416 | tf_op jit(solution)/shard_map/ppermute | solution.py:300
  187.9 0.6 copy.12
  (2 shorter events, 0.0 us)
Async XLA Ops:
  0.6 48.5 %copy-start.2 = (bf16[1,1024,256]{2,1,0:T(8,128)(2,1)S(1)}, bf16[1,1024,256]{2,1,0:T(8,128)(2,1)}, u32[]{:S(2)}) copy-start(bf16[1,1024,256]{2,1,0:T(8,128)(2,1)} %param.13) | copy-start | bytes 1572868
  0.6 48.5 %copy-start.1 = (bf16[1,256,1024]{2,1,0:T(8,128)(2,1)S(1)}, bf16[1,256,1024]{2,1,0:T(8,128)(2,1)}, u32[]{:S(2)}) copy-start(bf16[1,256,1024]{2,1,0:T(8,128)(2,1)} %param.12) | copy-start | bytes 1572868
  0.7 48.5 %copy-start = (bf16[1,256,1024]{2,1,0:T(8,128)(2,1)S(1)}, bf16[1,256,1024]{2,1,0:T(8,128)(2,1)}, u32[]{:S(2)}) copy-start(bf16[1,256,1024]{2,1,0:T(8,128)(2,1)} %param.11) | copy-start | bytes 1572868
  2.4 16.3 %collective-permute-start = (bf16[144,128]{1,0:T(8,128)(2,1)S(1)}, bf16[144,128]{1,0:T(8,128)(2,1)S(1)}, u32[]{:S(2)}, u32[]{:S(2)}) collective-permute-start(bf16[144,128]{1,0:T(8,128)(2,1)S(1)} %maximum_maximum_fusion), channel_id=1, source_target_pairs={{0,0},{1,1},{2,2},{3,3},{4,64},{5,65},{6,66},{7,67},{8,128},{9,129... | collective-permute-start | bytes 110600 | tf_op jit(solution)/shard_map/ppermute | solution.py:195
  50.5 56.3 %copy-start.3 = (f32[16,128]{1,0:T(8,128)S(1)}, f32[16,128]{1,0:T(8,128)}, u32[]{:S(2)}) copy-start(f32[16,128]{1,0:T(8,128)} %shard_map.102.weight_ref) | copy-start | bytes 24580
  107.1 10.7 %collective-permute-start.1 = (bf16[16,3072]{1,0:T(8,128)(2,1)S(1)}, bf16[16,3072]{1,0:T(8,128)(2,1)S(1)}, u32[]{:S(2)}, u32[]{:S(2)}) collective-permute-start(bf16[16,3072]{1,0:T(8,128)(2,1)S(1)} %shard_map.105), channel_id=1, source_target_pairs={{0,64},{64,0},{128,192},{192,128},{256,320},{320,256},{384,448},{4... | collective-permute-start | bytes 294920 | tf_op jit(solution)/shard_map/ppermute | solution.py:256
  117.8 10.7 %collective-permute-start.2 = (bf16[32,3072]{1,0:T(8,128)(2,1)S(1)}, bf16[32,3072]{1,0:T(8,128)(2,1)S(1)}, u32[]{:S(2)}, u32[]{:S(2)}) collective-permute-start(bf16[32,3072]{1,0:T(8,128)(2,1)S(1)} %pad_maximum_fusion.refs_1_), channel_id=1, source_target_pairs={{0,128},{1,897},{2,130},{3,899},{4,132},{5,901},{6,134},{7,903},{8... | collective-permute-start | bytes 589832 | tf_op jit(solution)/shard_map/ppermute | solution.py:260
  120.8 9.6 %collective-permute-start.3 = (bf16[32,3072]{1,0:T(8,128)(2,1)S(1)}, bf16[32,3072]{1,0:T(8,128)(2,1)S(1)}, u32[]{:S(2)}, u32[]{:S(2)}) collective-permute-start(bf16[32,3072]{1,0:T(8,128)(2,1)S(1)} %pad_maximum_fusion.refs_1_), channel_id=1, source_target_pairs={{0,896},{1,129},{2,898},{3,131},{4,900},{5,133},{6,902},{7,135},{8... | collective-permute-start | bytes 589832 | tf_op jit(solution)/shard_map/ppermute | solution.py:264
  128.5 8.9 %collective-permute-start.4 = (bf16[32,3072]{1,0:T(8,128)(2,1)S(1)}, bf16[32,3072]{1,0:T(8,128)(2,1)S(1)}, u32[]{:S(2)}, u32[]{:S(2)}) collective-permute-start(bf16[32,3072]{1,0:T(8,128)(2,1)S(1)} %collective-permute-done.2.refs_2_), channel_id=1, source_target_pairs={{0,128},{1,897},{2,130},{3,899},{4,132},{5,901},{6,134},{7,903},{8... | collective-permute-start | bytes 589832 | tf_op jit(solution)/shard_map/ppermute | solution.py:260
  130.4 9.2 %collective-permute-start.5 = (bf16[32,3072]{1,0:T(8,128)(2,1)S(1)}, bf16[32,3072]{1,0:T(8,128)(2,1)S(1)}, u32[]{:S(2)}, u32[]{:S(2)}) collective-permute-start(bf16[32,3072]{1,0:T(8,128)(2,1)S(1)} %collective-permute-done.3.refs_3_), channel_id=1, source_target_pairs={{0,896},{1,129},{2,898},{3,131},{4,900},{5,133},{6,902},{7,135},{8... | collective-permute-start | bytes 589832 | tf_op jit(solution)/shard_map/ppermute | solution.py:264
  137.4 8.1 %collective-permute-start.6 = (bf16[32,3072]{1,0:T(8,128)(2,1)S(1)}, bf16[32,3072]{1,0:T(8,128)(2,1)S(1)}, u32[]{:S(2)}, u32[]{:S(2)}) collective-permute-start(bf16[32,3072]{1,0:T(8,128)(2,1)S(1)} %collective-permute-done.4.refs_4_), channel_id=1, source_target_pairs={{0,128},{1,897},{2,130},{3,899},{4,132},{5,901},{6,134},{7,903},{8... | collective-permute-start | bytes 589832 | tf_op jit(solution)/shard_map/ppermute | solution.py:260
  139.6 8.4 %collective-permute-start.7 = (bf16[32,3072]{1,0:T(8,128)(2,1)S(1)}, bf16[32,3072]{1,0:T(8,128)(2,1)S(1)}, u32[]{:S(2)}, u32[]{:S(2)}) collective-permute-start(bf16[32,3072]{1,0:T(8,128)(2,1)S(1)} %collective-permute-done.5.refs_5_), channel_id=1, source_target_pairs={{0,896},{1,129},{2,898},{3,131},{4,900},{5,133},{6,902},{7,135},{8... | collective-permute-start | bytes 589832 | tf_op jit(solution)/shard_map/ppermute | solution.py:264
  145.6 7.8 %collective-permute-start.8 = (bf16[32,3072]{1,0:T(8,128)(2,1)S(1)}, bf16[32,3072]{1,0:T(8,128)(2,1)S(1)}, u32[]{:S(2)}, u32[]{:S(2)}) collective-permute-start(bf16[32,3072]{1,0:T(8,128)(2,1)S(1)} %collective-permute-done.6.refs_6_), channel_id=1, source_target_pairs={{0,128},{1,897},{2,130},{3,899},{4,132},{5,901},{6,134},{7,903},{8... | collective-permute-start | bytes 589832 | tf_op jit(solution)/shard_map/ppermute | solution.py:260
  172.6 15.2 %collective-permute-start.9 = (bf16[64,128]{1,0:T(8,128)(2,1)S(1)}, bf16[64,128]{1,0:T(8,128)(2,1)S(1)}, u32[]{:S(2)}, u32[]{:S(2)}) collective-permute-start(bf16[64,128]{1,0:T(8,128)(2,1)S(1)} %shard_map.107), channel_id=1, source_target_pairs={{0,0},{1,1},{2,2},{3,3},{64,4},{65,5},{66,6},{67,7},{128,8},{129,9... | collective-permute-start | bytes 49160 | tf_op jit(solution)/shard_map/ppermute | solution.py:300

commit v5 on v4

--- a/solution.py
+++ b/solution.py
@@ -254,16 +254,17 @@
         ]
 
     other = lax.ppermute(mine, "ep", [(b, b ^ 1) for b in range(blocks)])
-    right = left = jnp.concatenate([mine, other], axis=0)
-    steps, pieces = [0], [right]
-    for k in range(1, ring // 2 + 1):
-        right = lax.ppermute(right, ("ep", "edp"), shifted(1))
-        steps.append(-k)
-        pieces.append(right)
-        if k < ring - k:
-            left = lax.ppermute(left, ("ep", "edp"), shifted(-1))
-            steps.append(k)
-            pieces.append(left)
+    pair = jnp.concatenate([mine, other], axis=0)
+
+    def passed(piece, step):
+        return lax.ppermute(piece, ("ep", "edp"), shifted(step))
+
+    right_two, left_two = passed(pair, 2), passed(pair, -2)
+    right_one, left_one = passed(pair, 1), passed(pair, -1)
+    right_three, left_three = passed(right_two, 1), passed(left_two, -1)
+    steps = [0, -2, 2, -1, 1, -3, 3, -4]
+    pieces = [pair, right_two, left_two, right_one, left_one, right_three, left_three]
+    pieces.append(passed(right_two, 2))
 
     def slot_body(*refs):
         slot_grad_body(steps, *refs)

time: 189 us -> 182 us (0.963)
  waiting for transfers between devices: 29.7 us -> 23.1 us
  blocking collectives: 105 us -> 102 us
  starting transfers between devices: 43.6 us -> 46.2 us
    ppermute x7, waiting for transfers between devices: 13.7 us -> 7.5 us  [passed(): return lax.ppermute(piece, ('ep', 'edp'), shifted(step))]
    all_to_all x1, blocking collectives: 18.4 us -> 15.5 us  [per_device(): lax.all_to_all(slot_grad.reshape(experts, 8, 128), 'edp', split_axis=0, c...]
    ppermute x7, starting transfers between devices: 21.7 us -> 23.8 us  [passed(): return lax.ppermute(piece, ('ep', 'edp'), shifted(step))]
  transfers between devices with their start and end apart: 10 -> 10, of which waited for: 6 -> 7; matrix products, arithmetic and copies ran while one was open for 1% -> 1% of each run, Pallas kernels for 2% -> 2%
where the time goes in v5:
time: 182 us; the launch traced here: 181 us
  blocking collectives  102 us (56%)
  starting transfers between devices  46.2 us (25%)
  waiting for transfers between devices  23.1 us (13%)
  Pallas kernels  5.86 us (3%)
  other arithmetic  2.92 us (2%)
    all_to_all x1, blocking collectives, per_device(): lax.all_to_all(part.reshape(blocks, CAP, 3 * hid), 'ep', split_axis=0, co...  56.3 us
    all_to_all x1, blocking collectives, per_device(): lax.all_to_all(sent.reshape(experts, CAP, 2 * width), 'edp', split_axis=0...  30.1 us
    ppermute x7, starting transfers between devices, passed(): return lax.ppermute(piece, ('ep', 'edp'), shifted(step))  23.8 us
    all_to_all x1, blocking collectives, per_device(): lax.all_to_all(slot_grad.reshape(experts, 8, 128), 'edp', split_axis=0, c...  15.5 us
    ppermute x1, starting transfers between devices, per_device(): packed = lax.ppermute(packed, ('ep', 'edp'), there)  13.5 us
    ppermute x1, waiting for transfers between devices, per_device(): other = lax.ppermute(mine, 'ep', [(b, b ^ 1) for b in range(blocks)])  8.19 us
    ppermute x7, waiting for transfers between devices, passed(): return lax.ppermute(piece, ('ep', 'edp'), shifted(step))  7.5 us
    ppermute x1, waiting for transfers between devices, per_device(): token_grad = lax.ppermute(token_grad, ('ep', 'edp'), back).T  7.38 us
  transfers between devices with their start and end apart: 10, of which 7 were waited for; matrix products, arithmetic and copies ran while one was open for 1% of the time, Pallas kernels for 2%

profile of v5, /device:TPU:10, one launch (start us, length us, event | category | flops | bytes accessed | tf_op | source)
XLA Modules:
  0.0 181.5 jit_solution(13384103156054681638)
XLA Ops:
  0.6 0.0 copy-start.2
  0.6 0.0 copy-start.1
  0.7 0.0 copy-start
  0.7 0.8 convert_bitcast_fusion.1
  1.5 0.1 pad.5.clone
  1.6 0.8 maximum_maximum_fusion
  2.4 13.5 %collective-permute-start = (bf16[144,128]{1,0:T(8,128)(2,1)S(1)}, bf16[144,128]{1,0:T(8,128)(2,1)S(1)}, u32[]{:S(2)}, u32[]{:S(2)}) collective-permute-start(bf16[144,128]{1,0:T(8,128)(2,1)S(1)} %maximum_maximum_fusion), channel_id=1, source_target_pairs={{0,0},{1,1},{2,2},{3,3},{4,64},{5,65},{6,66},{7,67},{8,128},{9,129... | collective-permute-start | bytes 110600 | tf_op jit(solution)/shard_map/ppermute | solution.py:195
  15.9 1.3 convert_bitcast_fusion.mine_ref
  17.2 1.5 shard_map.102.weight_ref
  18.7 0.0 collective-permute-done.refs_0_
  18.7 0.4 shard_map.103
  19.1 30.1 %all_to_all.15 = bf16[64,16,128]{2,1,0:T(8,128)(2,1)S(1)} all-to-all(bf16[64,16,128]{2,1,0:T(8,128)(2,1)S(1)} %bitcast.33), channel_id=1, replica_groups=mesh['ep'=16,'edp'=64] {'edp'}, dimensions={0} | all-to-all | bytes 524288 | tf_op jit(solution)/shard_map/all_to_all | solution.py:218
  49.2 0.0 copy-done.2
  49.2 0.0 copy-done.1
  49.2 0.0 copy-done
  49.2 1.3 shard_map.104
  50.5 0.0 copy-start.3
  50.5 56.3 %all_to_all.16 = bf16[16,16,3072]{2,1,0:T(8,128)(2,1)S(1)} all-to-all(bf16[16,16,3072]{2,1,0:T(8,128)(2,1)S(1)} %bitcast.30), channel_id=1, replica_groups=mesh['ep'=16,'edp'=64] {'ep'}, dimensions={0} | all-to-all | bytes 3145728 | tf_op jit(solution)/shard_map/all_to_all | solution.py:238
  106.8 0.0 copy-done.3
  106.8 0.3 shard_map.105
  107.1 2.5 %collective-permute-start.1 = (bf16[16,3072]{1,0:T(8,128)(2,1)S(1)}, bf16[16,3072]{1,0:T(8,128)(2,1)S(1)}, u32[]{:S(2)}, u32[]{:S(2)}) collective-permute-start(bf16[16,3072]{1,0:T(8,128)(2,1)S(1)} %shard_map.105), channel_id=1, source_target_pairs={{0,64},{64,0},{128,192},{192,128},{256,320},{320,256},{384,448},{4... | collective-permute-start | bytes 294920 | tf_op jit(solution)/shard_map/ppermute | solution.py:256
  109.6 8.2 %collective-permute-done.1 = bf16[16,3072]{1,0:T(8,128)(2,1)S(1)} collective-permute-done((bf16[16,3072]{1,0:T(8,128)(2,1)S(1)}, bf16[16,3072]{1,0:T(8,128)(2,1)S(1)}, u32[]{:S(2)}, u32[]{:S(2)}) %collective-permute-start.1) | collective-permute-done | bytes 98336 | tf_op jit(solution)/shard_map/ppermute | solution.py:256
  117.8 5.2 %collective-permute-start.3 = (bf16[32,3072]{1,0:T(8,128)(2,1)S(1)}, bf16[32,3072]{1,0:T(8,128)(2,1)S(1)}, u32[]{:S(2)}, u32[]{:S(2)}) collective-permute-start(bf16[32,3072]{1,0:T(8,128)(2,1)S(1)} %pad_maximum_fusion.refs_1_), channel_id=1, source_target_pairs={{0,768},{1,257},{2,770},{3,259},{4,772},{5,261},{6,774},{7,263},{8... | collective-permute-start | bytes 589832 | tf_op jit(solution)/shard_map/ppermute | solution.py:260
  123.0 1.9 %collective-permute-start.2 = (bf16[32,3072]{1,0:T(8,128)(2,1)S(1)}, bf16[32,3072]{1,0:T(8,128)(2,1)S(1)}, u32[]{:S(2)}, u32[]{:S(2)}) collective-permute-start(bf16[32,3072]{1,0:T(8,128)(2,1)S(1)} %pad_maximum_fusion.refs_1_), channel_id=1, source_target_pairs={{0,256},{1,769},{2,258},{3,771},{4,260},{5,773},{6,262},{7,775},{8... | collective-permute-start | bytes 589832 | tf_op jit(solution)/shard_map/ppermute | solution.py:260
  125.0 4.7 %collective-permute-start.5 = (bf16[32,3072]{1,0:T(8,128)(2,1)S(1)}, bf16[32,3072]{1,0:T(8,128)(2,1)S(1)}, u32[]{:S(2)}, u32[]{:S(2)}) collective-permute-start(bf16[32,3072]{1,0:T(8,128)(2,1)S(1)} %pad_maximum_fusion.refs_1_), channel_id=1, source_target_pairs={{0,896},{1,129},{2,898},{3,131},{4,900},{5,133},{6,902},{7,135},{8... | collective-permute-start | bytes 589832 | tf_op jit(solution)/shard_map/ppermute | solution.py:260
  129.7 1.9 %collective-permute-start.4 = (bf16[32,3072]{1,0:T(8,128)(2,1)S(1)}, bf16[32,3072]{1,0:T(8,128)(2,1)S(1)}, u32[]{:S(2)}, u32[]{:S(2)}) collective-permute-start(bf16[32,3072]{1,0:T(8,128)(2,1)S(1)} %pad_maximum_fusion.refs_1_), channel_id=1, source_target_pairs={{0,128},{1,897},{2,130},{3,899},{4,132},{5,901},{6,134},{7,903},{8... | collective-permute-start | bytes 589832 | tf_op jit(solution)/shard_map/ppermute | solution.py:260
  131.6 0.8 collective-permute-done.3.refs_3_
  132.4 3.2 %collective-permute-start.7 = (bf16[32,3072]{1,0:T(8,128)(2,1)S(1)}, bf16[32,3072]{1,0:T(8,128)(2,1)S(1)}, u32[]{:S(2)}, u32[]{:S(2)}) collective-permute-start(bf16[32,3072]{1,0:T(8,128)(2,1)S(1)} %collective-permute-done.3.refs_3_), channel_id=1, source_target_pairs={{0,896},{1,129},{2,898},{3,131},{4,900},{5,133},{6,902},{7,135},{8... | collective-permute-start | bytes 589832 | tf_op jit(solution)/shard_map/ppermute | solution.py:260
  135.5 0.9 collective-permute-done.2.refs_2_
  136.5 3.2 %collective-permute-start.8 = (bf16[32,3072]{1,0:T(8,128)(2,1)S(1)}, bf16[32,3072]{1,0:T(8,128)(2,1)S(1)}, u32[]{:S(2)}, u32[]{:S(2)}) collective-permute-start(bf16[32,3072]{1,0:T(8,128)(2,1)S(1)} %collective-permute-done.2.refs_2_), channel_id=1, source_target_pairs={{0,256},{1,769},{2,258},{3,771},{4,260},{5,773},{6,262},{7,775},{8... | collective-permute-start | bytes 589832 | tf_op jit(solution)/shard_map/ppermute | solution.py:260
  139.6 3.8 %collective-permute-start.6 = (bf16[32,3072]{1,0:T(8,128)(2,1)S(1)}, bf16[32,3072]{1,0:T(8,128)(2,1)S(1)}, u32[]{:S(2)}, u32[]{:S(2)}) collective-permute-start(bf16[32,3072]{1,0:T(8,128)(2,1)S(1)} %collective-permute-done.2.refs_2_), channel_id=1, source_target_pairs={{0,128},{1,897},{2,130},{3,899},{4,132},{5,901},{6,134},{7,903},{8... | collective-permute-start | bytes 589832 | tf_op jit(solution)/shard_map/ppermute | solution.py:260
  143.4 0.0 collective-permute-done.5.refs_5_
  143.4 0.0 collective-permute-done.4.refs_4_
  143.5 0.4 collective-permute-done.7.refs_7_
  143.8 2.4 %collective-permute-done.8.refs_8_ = bf16[32,3072]{1,0:T(8,128)(2,1)S(1)} collective-permute-done((bf16[32,3072]{1,0:T(8,128)(2,1)S(1)}, bf16[32,3072]{1,0:T(8,128)(2,1)S(1)}, u32[]{:S(2)}, u32[]{:S(2)}) %collective-permute-start.8) | collective-permute-done | bytes 196640 | tf_op jit(solution)/shard_map/ppermute | solution.py:260
  146.2 3.0 %collective-permute-done.6.refs_6_ = bf16[32,3072]{1,0:T(8,128)(2,1)S(1)} collective-permute-done((bf16[32,3072]{1,0:T(8,128)(2,1)S(1)}, bf16[32,3072]{1,0:T(8,128)(2,1)S(1)}, u32[]{:S(2)}, u32[]{:S(2)}) %collective-permute-start.6) | collective-permute-done | bytes 196640 | tf_op jit(solution)/shard_map/ppermute | solution.py:260
  149.2 0.6 shard_map.106
  149.9 15.5 %all_to_all.17 = bf16[64,8,128]{2,1,0:T(8,128)(2,1)S(1)} all-to-all(bf16[64,8,128]{2,1,0:T(8,128)(2,1)S(1)} %bitcast.34), channel_id=1, replica_groups=mesh['ep'=16,'edp'=64] {'edp'}, dimensions={0} | all-to-all | bytes 262144 | tf_op jit(solution)/shard_map/all_to_all | solution.py:284
  165.4 0.3 shard_map.107
  165.6 6.4 %collective-permute-start.9 = (bf16[64,128]{1,0:T(8,128)(2,1)S(1)}, bf16[64,128]{1,0:T(8,128)(2,1)S(1)}, u32[]{:S(2)}, u32[]{:S(2)}) collective-permute-start(bf16[64,128]{1,0:T(8,128)(2,1)S(1)} %shard_map.107), channel_id=1, source_target_pairs={{0,0},{1,1},{2,2},{3,3},{64,4},{65,5},{66,6},{67,7},{128,8},{129,9... | collective-permute-start | bytes 49160 | tf_op jit(solution)/shard_map/ppermute | solution.py:301
  172.0 1.5 shard_map.108
  173.5 7.4 %collective-permute-done.9 = bf16[64,128]{1,0:T(8,128)(2,1)S(1)} collective-permute-done((bf16[64,128]{1,0:T(8,128)(2,1)S(1)}, bf16[64,128]{1,0:T(8,128)(2,1)S(1)}, u32[]{:S(2)}, u32[]{:S(2)}) %collective-permute-start.9) | collective-permute-done | bytes 16416 | tf_op jit(solution)/shard_map/ppermute | solution.py:301
  180.9 0.6 copy.12
  (2 shorter events, 0.0 us)
Async XLA Ops:
  0.6 48.5 %copy-start.2 = (bf16[1,1024,256]{2,1,0:T(8,128)(2,1)S(1)}, bf16[1,1024,256]{2,1,0:T(8,128)(2,1)}, u32[]{:S(2)}) copy-start(bf16[1,1024,256]{2,1,0:T(8,128)(2,1)} %param.13) | copy-start | bytes 1572868
  0.6 48.5 %copy-start.1 = (bf16[1,256,1024]{2,1,0:T(8,128)(2,1)S(1)}, bf16[1,256,1024]{2,1,0:T(8,128)(2,1)}, u32[]{:S(2)}) copy-start(bf16[1,256,1024]{2,1,0:T(8,128)(2,1)} %param.12) | copy-start | bytes 1572868
  0.7 48.5 %copy-start = (bf16[1,256,1024]{2,1,0:T(8,128)(2,1)S(1)}, bf16[1,256,1024]{2,1,0:T(8,128)(2,1)}, u32[]{:S(2)}) copy-start(bf16[1,256,1024]{2,1,0:T(8,128)(2,1)} %param.11) | copy-start | bytes 1572868
  2.4 16.3 %collective-permute-start = (bf16[144,128]{1,0:T(8,128)(2,1)S(1)}, bf16[144,128]{1,0:T(8,128)(2,1)S(1)}, u32[]{:S(2)}, u32[]{:S(2)}) collective-permute-start(bf16[144,128]{1,0:T(8,128)(2,1)S(1)} %maximum_maximum_fusion), channel_id=1, source_target_pairs={{0,0},{1,1},{2,2},{3,3},{4,64},{5,65},{6,66},{7,67},{8,128},{9,129... | collective-permute-start | bytes 110600 | tf_op jit(solution)/shard_map/ppermute | solution.py:195
  50.5 56.3 %copy-start.3 = (f32[16,128]{1,0:T(8,128)S(1)}, f32[16,128]{1,0:T(8,128)}, u32[]{:S(2)}) copy-start(f32[16,128]{1,0:T(8,128)} %shard_map.102.weight_ref) | copy-start | bytes 24580
  107.1 10.7 %collective-permute-start.1 = (bf16[16,3072]{1,0:T(8,128)(2,1)S(1)}, bf16[16,3072]{1,0:T(8,128)(2,1)S(1)}, u32[]{:S(2)}, u32[]{:S(2)}) collective-permute-start(bf16[16,3072]{1,0:T(8,128)(2,1)S(1)} %shard_map.105), channel_id=1, source_target_pairs={{0,64},{64,0},{128,192},{192,128},{256,320},{320,256},{384,448},{4... | collective-permute-start | bytes 294920 | tf_op jit(solution)/shard_map/ppermute | solution.py:256
  117.8 14.5 %collective-permute-start.3 = (bf16[32,3072]{1,0:T(8,128)(2,1)S(1)}, bf16[32,3072]{1,0:T(8,128)(2,1)S(1)}, u32[]{:S(2)}, u32[]{:S(2)}) collective-permute-start(bf16[32,3072]{1,0:T(8,128)(2,1)S(1)} %pad_maximum_fusion.refs_1_), channel_id=1, source_target_pairs={{0,768},{1,257},{2,770},{3,259},{4,772},{5,261},{6,774},{7,263},{8... | collective-permute-start | bytes 589832 | tf_op jit(solution)/shard_map/ppermute | solution.py:260
  123.0 13.4 %collective-permute-start.2 = (bf16[32,3072]{1,0:T(8,128)(2,1)S(1)}, bf16[32,3072]{1,0:T(8,128)(2,1)S(1)}, u32[]{:S(2)}, u32[]{:S(2)}) collective-permute-start(bf16[32,3072]{1,0:T(8,128)(2,1)S(1)} %pad_maximum_fusion.refs_1_), channel_id=1, source_target_pairs={{0,256},{1,769},{2,258},{3,771},{4,260},{5,773},{6,262},{7,775},{8... | collective-permute-start | bytes 589832 | tf_op jit(solution)/shard_map/ppermute | solution.py:260
  125.0 18.5 %collective-permute-start.5 = (bf16[32,3072]{1,0:T(8,128)(2,1)S(1)}, bf16[32,3072]{1,0:T(8,128)(2,1)S(1)}, u32[]{:S(2)}, u32[]{:S(2)}) collective-permute-start(bf16[32,3072]{1,0:T(8,128)(2,1)S(1)} %pad_maximum_fusion.refs_1_), channel_id=1, source_target_pairs={{0,896},{1,129},{2,898},{3,131},{4,900},{5,133},{6,902},{7,135},{8... | collective-permute-start | bytes 589832 | tf_op jit(solution)/shard_map/ppermute | solution.py:260
  129.7 13.8 %collective-permute-start.4 = (bf16[32,3072]{1,0:T(8,128)(2,1)S(1)}, bf16[32,3072]{1,0:T(8,128)(2,1)S(1)}, u32[]{:S(2)}, u32[]{:S(2)}) collective-permute-start(bf16[32,3072]{1,0:T(8,128)(2,1)S(1)} %pad_maximum_fusion.refs_1_), channel_id=1, source_target_pairs={{0,128},{1,897},{2,130},{3,899},{4,132},{5,901},{6,134},{7,903},{8... | collective-permute-start | bytes 589832 | tf_op jit(solution)/shard_map/ppermute | solution.py:260
  132.4 11.5 %collective-permute-start.7 = (bf16[32,3072]{1,0:T(8,128)(2,1)S(1)}, bf16[32,3072]{1,0:T(8,128)(2,1)S(1)}, u32[]{:S(2)}, u32[]{:S(2)}) collective-permute-start(bf16[32,3072]{1,0:T(8,128)(2,1)S(1)} %collective-permute-done.3.refs_3_), channel_id=1, source_target_pairs={{0,896},{1,129},{2,898},{3,131},{4,900},{5,133},{6,902},{7,135},{8... | collective-permute-start | bytes 589832 | tf_op jit(solution)/shard_map/ppermute | solution.py:260
  136.5 9.8 %collective-permute-start.8 = (bf16[32,3072]{1,0:T(8,128)(2,1)S(1)}, bf16[32,3072]{1,0:T(8,128)(2,1)S(1)}, u32[]{:S(2)}, u32[]{:S(2)}) collective-permute-start(bf16[32,3072]{1,0:T(8,128)(2,1)S(1)} %collective-permute-done.2.refs_2_), channel_id=1, source_target_pairs={{0,256},{1,769},{2,258},{3,771},{4,260},{5,773},{6,262},{7,775},{8... | collective-permute-start | bytes 589832 | tf_op jit(solution)/shard_map/ppermute | solution.py:260
  139.6 9.6 %collective-permute-start.6 = (bf16[32,3072]{1,0:T(8,128)(2,1)S(1)}, bf16[32,3072]{1,0:T(8,128)(2,1)S(1)}, u32[]{:S(2)}, u32[]{:S(2)}) collective-permute-start(bf16[32,3072]{1,0:T(8,128)(2,1)S(1)} %collective-permute-done.2.refs_2_), channel_id=1, source_target_pairs={{0,128},{1,897},{2,130},{3,899},{4,132},{5,901},{6,134},{7,903},{8... | collective-permute-start | bytes 589832 | tf_op jit(solution)/shard_map/ppermute | solution.py:260
  165.6 15.2 %collective-permute-start.9 = (bf16[64,128]{1,0:T(8,128)(2,1)S(1)}, bf16[64,128]{1,0:T(8,128)(2,1)S(1)}, u32[]{:S(2)}, u32[]{:S(2)}) collective-permute-start(bf16[64,128]{1,0:T(8,128)(2,1)S(1)} %shard_map.107), channel_id=1, source_target_pairs={{0,0},{1,1},{2,2},{3,3},{64,4},{65,5},{66,6},{67,7},{128,8},{129,9... | collective-permute-start | bytes 49160 | tf_op jit(solution)/shard_map/ppermute | solution.py:301

commit v6 on v5

--- a/solution.py
+++ b/solution.py
@@ -51,8 +51,8 @@
     ).astype(BF16)
 
 
-def weight_body(mine_ref, probs_ref, gate_ref, up_ref, down_ref, out_ref):
-    mine = mine_ref[...]
+def weight_body(experts, place_ref, ids_ref, probs_ref, gate_ref, up_ref, down_ref, out_ref):
+    mine = jnp.where(ids_ref[...] == lax.rem(place_ref[0], experts), 1.0, 0.0)
     toks = mine.shape[1]
     mask = jnp.sum(mine, axis=0, keepdims=True)
     weight = jnp.sum(mine * probs_ref[...], axis=0, keepdims=True)
@@ -116,18 +116,20 @@
     grads_ref[:, 2 * hid : 3 * hid] = hidden_weighted
 
 
-def slot_grad_body(steps, place_ref, *refs):
+def slot_grad_body(experts, steps, place_ref, *refs):
     pieces, (gate_ref, up_ref, out_ref, grads_ref) = refs[:-4], refs[-4:]
     hid = gate_ref.shape[1]
-    ring = len(steps)
-    spot = lax.div(place_ref[0], 4)
-    side = lax.rem(lax.div(place_ref[0], 2), 2)
+    ring = sum(len(held) for held in steps)
+    spot = lax.div(place_ref[0], 2 * experts)
+    side = lax.rem(lax.div(place_ref[0], experts), 2)
     way = 1 - 2 * lax.rem(place_ref[0], 2)
-    for step, piece_ref in zip(steps, pieces, strict=True):
-        pair = 2 * CAP * lax.rem(spot + step * way + ring, ring)
-        for half, z in ((0, side), (1, 1 - side)):
-            row = pl.multiple_of(pair + CAP * z, CAP)
-            grads_ref[pl.ds(row, CAP), :] = piece_ref[half * CAP : (half + 1) * CAP, :]
+    for held, piece_ref in zip(steps, pieces, strict=True):
+        for at, step in enumerate(held):
+            pair = 2 * CAP * lax.rem(spot + step * way + ring, ring)
+            for half, z in ((0, side), (1, 1 - side)):
+                row = pl.multiple_of(pair + CAP * z, CAP)
+                low = (2 * at + half) * CAP
+                grads_ref[pl.ds(row, CAP), :] = piece_ref[low : low + CAP, :]
     slot_grad = lax.dot_general(
         grads_ref[:, 0:hid], gate_ref[...], LAST, preferred_element_type=F32
     ) + lax.dot_general(
@@ -194,14 +196,19 @@
     )
     packed = lax.ppermute(packed, ("ep", "edp"), there)
 
-    mine = (ids == lax.axis_index("edp")).astype(F32)
+    rank = jnp.full((1,), lax.axis_index(("ep", "edp")), jnp.int32)
+
+    def slot_weights(*refs):
+        weight_body(experts, *refs)
+
     weight = pl.pallas_call(
-        weight_body,
+        slot_weights,
         out_shape=arr((CAP, toks), F32),
-        in_specs=[pl.BlockSpec(memory_space=pltpu.VMEM)] * 2
+        in_specs=[pl.BlockSpec(memory_space=pltpu.SMEM)]
+        + [pl.BlockSpec(memory_space=pltpu.VMEM)] * 2
         + [pl.BlockSpec(memory_space=pl.ANY)] * 3,
         cost_estimate=pl.CostEstimate(flops=10**5, bytes_accessed=10**4, transcendentals=0),
-    )(mine, probs.T, gate, up, down)
+    )(rank, ids, probs.T, gate, up, down)
 
     packed, weight = lax.optimization_barrier((packed, weight))
 
@@ -260,22 +267,19 @@
         return lax.ppermute(piece, ("ep", "edp"), shifted(step))
 
     right_two, left_two = passed(pair, 2), passed(pair, -2)
-    right_one, left_one = passed(pair, 1), passed(pair, -1)
-    right_three, left_three = passed(right_two, 1), passed(left_two, -1)
-    steps = [0, -2, 2, -1, 1, -3, 3, -4]
-    pieces = [pair, right_two, left_two, right_one, left_one, right_three, left_three]
-    pieces.append(passed(right_two, 2))
+    right_on = passed(jnp.concatenate([right_two, pair], axis=0), 1)
+    left_on = passed(jnp.concatenate([left_two, pair], axis=0), -1)
+    steps = [(0,), (-2,), (2,), (-3, -1), (3, 1), (-4,)]
+    pieces = [pair, right_two, left_two, right_on, left_on, passed(right_two, 2)]
 
     def slot_body(*refs):
-        slot_grad_body(steps, *refs)
-
-    code = lax.axis_index("ep") * 2 + lax.rem(lax.axis_index("edp"), 2)
-    rank = jnp.full((1,), code, jnp.int32)
+        slot_grad_body(experts, steps, *refs)
+
     slot_grad, grads = pl.pallas_call(
         slot_body,
         out_shape=(arr((4 * slots // 2, 128)), arr((slots, 3 * hid))),
         in_specs=[pl.BlockSpec(memory_space=pltpu.SMEM)]
-        + [pl.BlockSpec(memory_space=pltpu.VMEM)] * (ring + 2),
+        + [pl.BlockSpec(memory_space=pltpu.VMEM)] * (len(pieces) + 2),
         compiler_params=pltpu.CompilerParams(vmem_limit_bytes=40 * 1024 * 1024),
         cost_estimate=pl.CostEstimate(
             flops=4 * slots * wide * hid, bytes_accessed=5 * 10**6, transcendentals=0

time: 182 us -> 186 us (1.022)
  waiting for transfers between devices: 23.1 us -> 39.1 us
  starting transfers between devices: 46.2 us -> 35.3 us
    ppermute x7 -> x5, waiting for transfers between devices: 7.5 us -> 20.7 us  [passed(): return lax.ppermute(piece, ('ep', 'edp'), shifted(step))]
    ppermute x7 -> x5, starting transfers between devices: 23.8 us -> 15.1 us  [passed(): return lax.ppermute(piece, ('ep', 'edp'), shifted(step))]
    ppermute x1, waiting for transfers between devices: 7.38 us -> 9.49 us  [per_device(): token_grad = lax.ppermute(token_grad, ('ep', 'edp'), back).T]
    ppermute x1, starting transfers between devices: 6.39 us -> 4.28 us  [per_device(): token_grad = lax.ppermute(token_grad, ('ep', 'edp'), back).T]
  transfers between devices with their start and end apart: 10 -> 8, of which waited for: 7 -> 6; matrix products, arithmetic and copies ran while one was open for 1% -> 0% of each run, Pallas kernels for 2% -> 2%
where the time goes in v6:
time: 186 us
  blocking collectives  102 us (55%)
  waiting for transfers between devices  39.1 us (21%)
  starting transfers between devices  35.3 us (19%)
  Pallas kernels  5.87 us (3%)
    all_to_all x1, blocking collectives, per_device(): lax.all_to_all(part.reshape(blocks, CAP, 3 * hid), 'ep', split_axis=0, co...  56.3 us
    all_to_all x1, blocking collectives, per_device(): lax.all_to_all(sent.reshape(experts, CAP, 2 * width), 'edp', split_axis=0...  30.6 us
    ppermute x5, waiting for transfers between devices, passed(): return lax.ppermute(piece, ('ep', 'edp'), shifted(step))  20.7 us
    all_to_all x1, blocking collectives, per_device(): lax.all_to_all(slot_grad.reshape(experts, 8, 128), 'edp', split_axis=0, c...  15.3 us
    ppermute x5, starting transfers between devices, passed(): return lax.ppermute(piece, ('ep', 'edp'), shifted(step))  15.1 us
    ppermute x1, starting transfers between devices, per_device(): packed = lax.ppermute(packed, ('ep', 'edp'), there)  13.5 us
    ppermute x1, waiting for transfers between devices, per_device(): token_grad = lax.ppermute(token_grad, ('ep', 'edp'), back).T  9.49 us
    ppermute x1, waiting for transfers between devices, per_device(): other = lax.ppermute(mine, 'ep', [(b, b ^ 1) for b in range(blocks)])  8.2 us
  transfers between devices with their start and end apart: 8, of which 6 were waited for; matrix products, arithmetic and copies ran while one was open for 0% of the time, Pallas kernels for 2%

profile of v6, /device:TPU:10, one launch (start us, length us, event | category | flops | bytes accessed | tf_op | source)
XLA Modules:
  0.0 185.8 jit_solution(10004581006323604211)
XLA Ops:
  0.6 0.0 copy-start.2
  0.6 0.0 copy-start.1
  0.7 0.0 copy-start
  0.7 0.8 bitcast_convert_fusion
  1.5 0.1 pad.11.clone
  1.6 0.8 maximum_maximum_fusion
  2.4 13.5 %collective-permute-start = (bf16[144,128]{1,0:T(8,128)(2,1)S(1)}, bf16[144,128]{1,0:T(8,128)(2,1)S(1)}, u32[]{:S(2)}, u32[]{:S(2)}) collective-permute-start(bf16[144,128]{1,0:T(8,128)(2,1)S(1)} %maximum_maximum_fusion), channel_id=1, source_target_pairs={{0,0},{1,1},{2,2},{3,3},{4,64},{5,65},{6,66},{7,67},{8,128},{9,129... | collective-permute-start | bytes 110600 | tf_op jit(solution)/shard_map/ppermute | solution.py:197
  15.9 1.5 shard_map.102.weight_ref
  17.4 0.7 collective-permute-done.refs_0_
  18.1 0.4 shard_map.103
  18.5 30.6 %all_to_all.15 = bf16[64,16,128]{2,1,0:T(8,128)(2,1)S(1)} all-to-all(bf16[64,16,128]{2,1,0:T(8,128)(2,1)S(1)} %bitcast.31), channel_id=1, replica_groups=mesh['ep'=16,'edp'=64] {'edp'}, dimensions={0} | all-to-all | bytes 524288 | tf_op jit(solution)/shard_map/all_to_all | solution.py:225
  49.2 0.0 copy-done.2
  49.2 0.0 copy-done.1
  49.2 0.0 copy-done
  49.2 1.3 shard_map.104
  50.5 0.0 copy-start.3
  50.5 56.3 %all_to_all.16 = bf16[16,16,3072]{2,1,0:T(8,128)(2,1)S(1)} all-to-all(bf16[16,16,3072]{2,1,0:T(8,128)(2,1)S(1)} %bitcast.28), channel_id=1, replica_groups=mesh['ep'=16,'edp'=64] {'ep'}, dimensions={0} | all-to-all | bytes 3145728 | tf_op jit(solution)/shard_map/all_to_all | solution.py:245
  106.8 0.0 copy-done.3
  106.8 0.3 shard_map.105
  107.1 2.5 %collective-permute-start.1 = (bf16[16,3072]{1,0:T(8,128)(2,1)S(1)}, bf16[16,3072]{1,0:T(8,128)(2,1)S(1)}, u32[]{:S(2)}, u32[]{:S(2)}) collective-permute-start(bf16[16,3072]{1,0:T(8,128)(2,1)S(1)} %shard_map.105), channel_id=1, source_target_pairs={{0,64},{64,0},{128,192},{192,128},{256,320},{320,256},{384,448},{4... | collective-permute-start | bytes 294920 | tf_op jit(solution)/shard_map/ppermute | solution.py:263
  109.6 8.2 %collective-permute-done.1 = bf16[16,3072]{1,0:T(8,128)(2,1)S(1)} collective-permute-done((bf16[16,3072]{1,0:T(8,128)(2,1)S(1)}, bf16[16,3072]{1,0:T(8,128)(2,1)S(1)}, u32[]{:S(2)}, u32[]{:S(2)}) %collective-permute-start.1) | collective-permute-done | bytes 98336 | tf_op jit(solution)/shard_map/ppermute | solution.py:263
  117.8 5.2 %collective-permute-start.3 = (bf16[32,3072]{1,0:T(8,128)(2,1)S(1)}, bf16[32,3072]{1,0:T(8,128)(2,1)S(1)}, u32[]{:S(2)}, u32[]{:S(2)}) collective-permute-start(bf16[32,3072]{1,0:T(8,128)(2,1)S(1)} %pad_maximum_fusion.4.refs_1_), channel_id=1, source_target_pairs={{0,768},{1,257},{2,770},{3,259},{4,772},{5,261},{6,774},{7,263},{8... | collective-permute-start | bytes 589832 | tf_op jit(solution)/shard_map/ppermute | solution.py:267
  123.0 1.9 %collective-permute-start.2 = (bf16[32,3072]{1,0:T(8,128)(2,1)S(1)}, bf16[32,3072]{1,0:T(8,128)(2,1)S(1)}, u32[]{:S(2)}, u32[]{:S(2)}) collective-permute-start(bf16[32,3072]{1,0:T(8,128)(2,1)S(1)} %pad_maximum_fusion.4.refs_1_), channel_id=1, source_target_pairs={{0,256},{1,769},{2,258},{3,771},{4,260},{5,773},{6,262},{7,775},{8... | collective-permute-start | bytes 589832 | tf_op jit(solution)/shard_map/ppermute | solution.py:267
  125.0 7.1 %collective-permute-done.3.refs_3_ = bf16[32,3072]{1,0:T(8,128)(2,1)S(1)} collective-permute-done((bf16[32,3072]{1,0:T(8,128)(2,1)S(1)}, bf16[32,3072]{1,0:T(8,128)(2,1)S(1)}, u32[]{:S(2)}, u32[]{:S(2)}) %collective-permute-start.3) | collective-permute-done | bytes 196640 | tf_op jit(solution)/shard_map/ppermute | solution.py:267
  132.0 2.1 %collective-permute-done.2.refs_2_ = bf16[32,3072]{1,0:T(8,128)(2,1)S(1)} collective-permute-done((bf16[32,3072]{1,0:T(8,128)(2,1)S(1)}, bf16[32,3072]{1,0:T(8,128)(2,1)S(1)}, u32[]{:S(2)}, u32[]{:S(2)}) %collective-permute-start.2) | collective-permute-done | bytes 196640 | tf_op jit(solution)/shard_map/ppermute | solution.py:267
  134.1 0.1 pad_maximum_fusion
  134.2 1.9 %collective-permute-start.5 = (bf16[64,3072]{1,0:T(8,128)(2,1)S(1)}, bf16[64,3072]{1,0:T(8,128)(2,1)S(1)}, u32[]{:S(2)}, u32[]{:S(2)}) collective-permute-start(bf16[64,3072]{1,0:T(8,128)(2,1)S(1)} %get-tuple-element.32), channel_id=1, source_target_pairs={{0,896},{1,129},{2,898},{3,131},{4,900},{5,133},{6,902},{7,135},{8... | collective-permute-start | bytes 1179656 | tf_op jit(solution)/shard_map/ppermute | solution.py:267
  136.1 3.9 %collective-permute-start.4 = (bf16[64,3072]{1,0:T(8,128)(2,1)S(1)}, bf16[64,3072]{1,0:T(8,128)(2,1)S(1)}, u32[]{:S(2)}, u32[]{:S(2)}) collective-permute-start(bf16[64,3072]{1,0:T(8,128)(2,1)S(1)} %get-tuple-element.33), channel_id=1, source_target_pairs={{0,128},{1,897},{2,130},{3,899},{4,132},{5,901},{6,134},{7,903},{8... | collective-permute-start | bytes 1179656 | tf_op jit(solution)/shard_map/ppermute | solution.py:267
  140.0 2.1 %collective-permute-start.6 = (bf16[32,3072]{1,0:T(8,128)(2,1)S(1)}, bf16[32,3072]{1,0:T(8,128)(2,1)S(1)}, u32[]{:S(2)}, u32[]{:S(2)}) collective-permute-start(bf16[32,3072]{1,0:T(8,128)(2,1)S(1)} %collective-permute-done.2.refs_2_), channel_id=1, source_target_pairs={{0,256},{1,769},{2,258},{3,771},{4,260},{5,773},{6,262},{7,775},{8... | collective-permute-start | bytes 589832 | tf_op jit(solution)/shard_map/ppermute | solution.py:267
  142.2 11.5 %collective-permute-done.6.refs_6_ = bf16[32,3072]{1,0:T(8,128)(2,1)S(1)} collective-permute-done((bf16[32,3072]{1,0:T(8,128)(2,1)S(1)}, bf16[32,3072]{1,0:T(8,128)(2,1)S(1)}, u32[]{:S(2)}, u32[]{:S(2)}) %collective-permute-start.6) | collective-permute-done | bytes 196640 | tf_op jit(solution)/shard_map/ppermute | solution.py:267
  153.7 0.0 collective-permute-done.5.refs_5_
  153.7 0.0 collective-permute-done.4.refs_4_
  153.7 0.6 shard_map.106
  154.3 15.3 %all_to_all.17 = bf16[64,8,128]{2,1,0:T(8,128)(2,1)S(1)} all-to-all(bf16[64,8,128]{2,1,0:T(8,128)(2,1)S(1)} %bitcast.32), channel_id=1, replica_groups=mesh['ep'=16,'edp'=64] {'edp'}, dimensions={0} | all-to-all | bytes 262144 | tf_op jit(solution)/shard_map/all_to_all | solution.py:288
  169.6 0.3 shard_map.107
  169.9 4.3 %collective-permute-start.7 = (bf16[64,128]{1,0:T(8,128)(2,1)S(1)}, bf16[64,128]{1,0:T(8,128)(2,1)S(1)}, u32[]{:S(2)}, u32[]{:S(2)}) collective-permute-start(bf16[64,128]{1,0:T(8,128)(2,1)S(1)} %shard_map.107), channel_id=1, source_target_pairs={{0,0},{1,1},{2,2},{3,3},{64,4},{65,5},{66,6},{67,7},{128,8},{129,9... | collective-permute-start | bytes 49160 | tf_op jit(solution)/shard_map/ppermute | solution.py:305
  174.2 1.5 shard_map.108
  175.7 9.5 %collective-permute-done.7 = bf16[64,128]{1,0:T(8,128)(2,1)S(1)} collective-permute-done((bf16[64,128]{1,0:T(8,128)(2,1)S(1)}, bf16[64,128]{1,0:T(8,128)(2,1)S(1)}, u32[]{:S(2)}, u32[]{:S(2)}) %collective-permute-start.7) | collective-permute-done | bytes 16416 | tf_op jit(solution)/shard_map/ppermute | solution.py:305
  185.2 0.6 copy.12
  (2 shorter events, 0.0 us)
Async XLA Ops:
  0.6 48.5 %copy-start.2 = (bf16[1,1024,256]{2,1,0:T(8,128)(2,1)S(1)}, bf16[1,1024,256]{2,1,0:T(8,128)(2,1)}, u32[]{:S(2)}) copy-start(bf16[1,1024,256]{2,1,0:T(8,128)(2,1)} %param.13) | copy-start | bytes 1572868
  0.6 48.5 %copy-start.1 = (bf16[1,256,1024]{2,1,0:T(8,128)(2,1)S(1)}, bf16[1,256,1024]{2,1,0:T(8,128)(2,1)}, u32[]{:S(2)}) copy-start(bf16[1,256,1024]{2,1,0:T(8,128)(2,1)} %param.12) | copy-start | bytes 1572868
  0.7 48.5 %copy-start = (bf16[1,256,1024]{2,1,0:T(8,128)(2,1)S(1)}, bf16[1,256,1024]{2,1,0:T(8,128)(2,1)}, u32[]{:S(2)}) copy-start(bf16[1,256,1024]{2,1,0:T(8,128)(2,1)} %param.11) | copy-start | bytes 1572868
  2.4 15.8 %collective-permute-start = (bf16[144,128]{1,0:T(8,128)(2,1)S(1)}, bf16[144,128]{1,0:T(8,128)(2,1)S(1)}, u32[]{:S(2)}, u32[]{:S(2)}) collective-permute-start(bf16[144,128]{1,0:T(8,128)(2,1)S(1)} %maximum_maximum_fusion), channel_id=1, source_target_pairs={{0,0},{1,1},{2,2},{3,3},{4,64},{5,65},{6,66},{7,67},{8,128},{9,129... | collective-permute-start | bytes 110600 | tf_op jit(solution)/shard_map/ppermute | solution.py:197
  50.5 56.3 %copy-start.3 = (f32[16,128]{1,0:T(8,128)S(1)}, f32[16,128]{1,0:T(8,128)}, u32[]{:S(2)}) copy-start(f32[16,128]{1,0:T(8,128)} %shard_map.102.weight_ref) | copy-start | bytes 24580
  107.1 10.7 %collective-permute-start.1 = (bf16[16,3072]{1,0:T(8,128)(2,1)S(1)}, bf16[16,3072]{1,0:T(8,128)(2,1)S(1)}, u32[]{:S(2)}, u32[]{:S(2)}) collective-permute-start(bf16[16,3072]{1,0:T(8,128)(2,1)S(1)} %shard_map.105), channel_id=1, source_target_pairs={{0,64},{64,0},{128,192},{192,128},{256,320},{320,256},{384,448},{4... | collective-permute-start | bytes 294920 | tf_op jit(solution)/shard_map/ppermute | solution.py:263
  117.8 14.2 %collective-permute-start.3 = (bf16[32,3072]{1,0:T(8,128)(2,1)S(1)}, bf16[32,3072]{1,0:T(8,128)(2,1)S(1)}, u32[]{:S(2)}, u32[]{:S(2)}) collective-permute-start(bf16[32,3072]{1,0:T(8,128)(2,1)S(1)} %pad_maximum_fusion.4.refs_1_), channel_id=1, source_target_pairs={{0,768},{1,257},{2,770},{3,259},{4,772},{5,261},{6,774},{7,263},{8... | collective-permute-start | bytes 589832 | tf_op jit(solution)/shard_map/ppermute | solution.py:267
  123.0 11.1 %collective-permute-start.2 = (bf16[32,3072]{1,0:T(8,128)(2,1)S(1)}, bf16[32,3072]{1,0:T(8,128)(2,1)S(1)}, u32[]{:S(2)}, u32[]{:S(2)}) collective-permute-start(bf16[32,3072]{1,0:T(8,128)(2,1)S(1)} %pad_maximum_fusion.4.refs_1_), channel_id=1, source_target_pairs={{0,256},{1,769},{2,258},{3,771},{4,260},{5,773},{6,262},{7,775},{8... | collective-permute-start | bytes 589832 | tf_op jit(solution)/shard_map/ppermute | solution.py:267
  134.2 19.5 %collective-permute-start.5 = (bf16[64,3072]{1,0:T(8,128)(2,1)S(1)}, bf16[64,3072]{1,0:T(8,128)(2,1)S(1)}, u32[]{:S(2)}, u32[]{:S(2)}) collective-permute-start(bf16[64,3072]{1,0:T(8,128)(2,1)S(1)} %get-tuple-element.32), channel_id=1, source_target_pairs={{0,896},{1,129},{2,898},{3,131},{4,900},{5,133},{6,902},{7,135},{8... | collective-permute-start | bytes 1179656 | tf_op jit(solution)/shard_map/ppermute | solution.py:267
  136.1 17.6 %collective-permute-start.4 = (bf16[64,3072]{1,0:T(8,128)(2,1)S(1)}, bf16[64,3072]{1,0:T(8,128)(2,1)S(1)}, u32[]{:S(2)}, u32[]{:S(2)}) collective-permute-start(bf16[64,3072]{1,0:T(8,128)(2,1)S(1)} %get-tuple-element.33), channel_id=1, source_target_pairs={{0,128},{1,897},{2,130},{3,899},{4,132},{5,901},{6,134},{7,903},{8... | collective-permute-start | bytes 1179656 | tf_op jit(solution)/shard_map/ppermute | solution.py:267
  140.0 13.7 %collective-permute-start.6 = (bf16[32,3072]{1,0:T(8,128)(2,1)S(1)}, bf16[32,3072]{1,0:T(8,128)(2,1)S(1)}, u32[]{:S(2)}, u32[]{:S(2)}) collective-permute-start(bf16[32,3072]{1,0:T(8,128)(2,1)S(1)} %collective-permute-done.2.refs_2_), channel_id=1, source_target_pairs={{0,256},{1,769},{2,258},{3,771},{4,260},{5,773},{6,262},{7,775},{8... | collective-permute-start | bytes 589832 | tf_op jit(solution)/shard_map/ppermute | solution.py:267
  169.9 15.2 %collective-permute-start.7 = (bf16[64,128]{1,0:T(8,128)(2,1)S(1)}, bf16[64,128]{1,0:T(8,128)(2,1)S(1)}, u32[]{:S(2)}, u32[]{:S(2)}) collective-permute-start(bf16[64,128]{1,0:T(8,128)(2,1)S(1)} %shard_map.107), channel_id=1, source_target_pairs={{0,0},{1,1},{2,2},{3,3},{64,4},{65,5},{66,6},{67,7},{128,8},{129,9... | collective-permute-start | bytes 49160 | tf_op jit(solution)/shard_map/ppermute | solution.py:305

commit v7 on v6

--- a/solution.py
+++ b/solution.py
@@ -267,10 +267,11 @@
         return lax.ppermute(piece, ("ep", "edp"), shifted(step))
 
     right_two, left_two = passed(pair, 2), passed(pair, -2)
-    right_on = passed(jnp.concatenate([right_two, pair], axis=0), 1)
-    left_on = passed(jnp.concatenate([left_two, pair], axis=0), -1)
-    steps = [(0,), (-2,), (2,), (-3, -1), (3, 1), (-4,)]
-    pieces = [pair, right_two, left_two, right_on, left_on, passed(right_two, 2)]
+    right_one, left_one = passed(pair, 1), passed(pair, -1)
+    right_three, left_three = passed(right_two, 1), passed(left_two, -1)
+    steps = [(0,), (-2,), (2,), (-1,), (1,), (-3,), (3,), (-4,)]
+    pieces = [pair, right_two, left_two, right_one, left_one, right_three, left_three]
+    pieces.append(passed(right_two, 2))
 
     def slot_body(*refs):
         slot_grad_body(experts, steps, *refs)

time: 186 us -> 182 us (0.978)
  the two profiles are of different devices: /device:TPU:10 before, /device:TPU:38 now
where the time goes in v7:
time: 182 us
  blocking collectives  96.4 us (53%)
  starting transfers between devices  47.8 us (26%)
  waiting for transfers between devices  28.4 us (16%)
  Pallas kernels  5.88 us (3%)
    all_to_all x1, blocking collectives, per_device(): lax.all_to_all(part.reshape(blocks, CAP, 3 * hid), 'ep', split_axis=0, co...  58.2 us
    ppermute x7, starting transfers between devices, passed(): return lax.ppermute(piece, ('ep', 'edp'), shifted(step))  24 us
    all_to_all x1, blocking collectives, per_device(): lax.all_to_all(sent.reshape(experts, CAP, 2 * width), 'edp', split_axis=0...  22.5 us
    ppermute x1, starting transfers between devices, per_device(): packed = lax.ppermute(packed, ('ep', 'edp'), there)  18.9 us
    all_to_all x1, blocking collectives, per_device(): lax.all_to_all(slot_grad.reshape(experts, 8, 128), 'edp', split_axis=0, c...  15.6 us
    ppermute x1, waiting for transfers between devices, per_device(): token_grad = lax.ppermute(token_grad, ('ep', 'edp'), back).T  10.8 us
    ppermute x1, waiting for transfers between devices, per_device(): other = lax.ppermute(mine, 'ep', [(b, b ^ 1) for b in range(blocks)])  9.96 us
    ppermute x7, waiting for transfers between devices, passed(): return lax.ppermute(piece, ('ep', 'edp'), shifted(step))  6.96 us
  transfers between devices with their start and end apart: 10, of which 6 were waited for; matrix products, arithmetic and copies ran while one was open for 0% of the time, Pallas kernels for 2%

profile of v7, /device:TPU:38, one launch (start us, length us, event | category | flops | bytes accessed | tf_op | source)
XLA Modules:
  0.0 181.6 jit_solution(15742603135028533750)
XLA Ops:
  0.6 0.0 copy-start.2
  0.6 0.0 copy-start.1
  0.7 0.0 copy-start
  0.7 0.8 bitcast_convert_fusion
  1.5 0.1 pad.5.clone
  1.6 0.8 maximum_maximum_fusion
  2.4 18.9 %collective-permute-start = (bf16[144,128]{1,0:T(8,128)(2,1)S(1)}, bf16[144,128]{1,0:T(8,128)(2,1)S(1)}, u32[]{:S(2)}, u32[]{:S(2)}) collective-permute-start(bf16[144,128]{1,0:T(8,128)(2,1)S(1)} %maximum_maximum_fusion), channel_id=1, source_target_pairs={{0,0},{1,1},{2,2},{3,3},{4,64},{5,65},{6,66},{7,67},{8,128},{9,129... | collective-permute-start | bytes 110600 | tf_op jit(solution)/shard_map/ppermute | solution.py:197
  21.2 1.5 shard_map.102.weight_ref
  22.8 0.7 collective-permute-done.refs_0_
  23.5 0.4 shard_map.103
  23.9 22.5 %all_to_all.15 = bf16[64,16,128]{2,1,0:T(8,128)(2,1)S(1)} all-to-all(bf16[64,16,128]{2,1,0:T(8,128)(2,1)S(1)} %bitcast.31), channel_id=1, replica_groups=mesh['ep'=16,'edp'=64] {'edp'}, dimensions={0} | all-to-all | bytes 524288 | tf_op jit(solution)/shard_map/all_to_all | solution.py:225
  46.4 0.0 copy-done.2
  46.4 0.0 copy-done.1
  46.4 0.0 copy-done
  46.4 1.3 shard_map.104
  47.7 0.0 copy-start.3
  47.7 58.2 %all_to_all.16 = bf16[16,16,3072]{2,1,0:T(8,128)(2,1)S(1)} all-to-all(bf16[16,16,3072]{2,1,0:T(8,128)(2,1)S(1)} %bitcast.28), channel_id=1, replica_groups=mesh['ep'=16,'edp'=64] {'ep'}, dimensions={0} | all-to-all | bytes 3145728 | tf_op jit(solution)/shard_map/all_to_all | solution.py:245
  105.9 0.0 copy-done.3
  105.9 0.3 shard_map.105
  106.3 2.3 %collective-permute-start.1 = (bf16[16,3072]{1,0:T(8,128)(2,1)S(1)}, bf16[16,3072]{1,0:T(8,128)(2,1)S(1)}, u32[]{:S(2)}, u32[]{:S(2)}) collective-permute-start(bf16[16,3072]{1,0:T(8,128)(2,1)S(1)} %shard_map.105), channel_id=1, source_target_pairs={{0,64},{64,0},{128,192},{192,128},{256,320},{320,256},{384,448},{4... | collective-permute-start | bytes 294920 | tf_op jit(solution)/shard_map/ppermute | solution.py:263
  108.5 10.0 %collective-permute-done.1 = bf16[16,3072]{1,0:T(8,128)(2,1)S(1)} collective-permute-done((bf16[16,3072]{1,0:T(8,128)(2,1)S(1)}, bf16[16,3072]{1,0:T(8,128)(2,1)S(1)}, u32[]{:S(2)}, u32[]{:S(2)}) %collective-permute-start.1) | collective-permute-done | bytes 98336 | tf_op jit(solution)/shard_map/ppermute | solution.py:263
  118.5 1.9 %collective-permute-start.3 = (bf16[32,3072]{1,0:T(8,128)(2,1)S(1)}, bf16[32,3072]{1,0:T(8,128)(2,1)S(1)}, u32[]{:S(2)}, u32[]{:S(2)}) collective-permute-start(bf16[32,3072]{1,0:T(8,128)(2,1)S(1)} %pad_maximum_fusion.refs_1_), channel_id=1, source_target_pairs={{0,768},{1,257},{2,770},{3,259},{4,772},{5,261},{6,774},{7,263},{8... | collective-permute-start | bytes 589832 | tf_op jit(solution)/shard_map/ppermute | solution.py:267
  120.4 6.0 %collective-permute-start.2 = (bf16[32,3072]{1,0:T(8,128)(2,1)S(1)}, bf16[32,3072]{1,0:T(8,128)(2,1)S(1)}, u32[]{:S(2)}, u32[]{:S(2)}) collective-permute-start(bf16[32,3072]{1,0:T(8,128)(2,1)S(1)} %pad_maximum_fusion.refs_1_), channel_id=1, source_target_pairs={{0,256},{1,769},{2,258},{3,771},{4,260},{5,773},{6,262},{7,775},{8... | collective-permute-start | bytes 589832 | tf_op jit(solution)/shard_map/ppermute | solution.py:267
  126.5 1.9 %collective-permute-start.5 = (bf16[32,3072]{1,0:T(8,128)(2,1)S(1)}, bf16[32,3072]{1,0:T(8,128)(2,1)S(1)}, u32[]{:S(2)}, u32[]{:S(2)}) collective-permute-start(bf16[32,3072]{1,0:T(8,128)(2,1)S(1)} %pad_maximum_fusion.refs_1_), channel_id=1, source_target_pairs={{0,896},{1,129},{2,898},{3,131},{4,900},{5,133},{6,902},{7,135},{8... | collective-permute-start | bytes 589832 | tf_op jit(solution)/shard_map/ppermute | solution.py:267
  128.4 5.1 %collective-permute-start.4 = (bf16[32,3072]{1,0:T(8,128)(2,1)S(1)}, bf16[32,3072]{1,0:T(8,128)(2,1)S(1)}, u32[]{:S(2)}, u32[]{:S(2)}) collective-permute-start(bf16[32,3072]{1,0:T(8,128)(2,1)S(1)} %pad_maximum_fusion.refs_1_), channel_id=1, source_target_pairs={{0,128},{1,897},{2,130},{3,899},{4,132},{5,901},{6,134},{7,903},{8... | collective-permute-start | bytes 589832 | tf_op jit(solution)/shard_map/ppermute | solution.py:267
  133.5 0.8 collective-permute-done.3.refs_3_
  134.4 1.9 %collective-permute-start.7 = (bf16[32,3072]{1,0:T(8,128)(2,1)S(1)}, bf16[32,3072]{1,0:T(8,128)(2,1)S(1)}, u32[]{:S(2)}, u32[]{:S(2)}) collective-permute-start(bf16[32,3072]{1,0:T(8,128)(2,1)S(1)} %collective-permute-done.3.refs_3_), channel_id=1, source_target_pairs={{0,896},{1,129},{2,898},{3,131},{4,900},{5,133},{6,902},{7,135},{8... | collective-permute-start | bytes 589832 | tf_op jit(solution)/shard_map/ppermute | solution.py:267
  136.3 0.0 collective-permute-done.2.refs_2_
  136.3 3.3 %collective-permute-start.8 = (bf16[32,3072]{1,0:T(8,128)(2,1)S(1)}, bf16[32,3072]{1,0:T(8,128)(2,1)S(1)}, u32[]{:S(2)}, u32[]{:S(2)}) collective-permute-start(bf16[32,3072]{1,0:T(8,128)(2,1)S(1)} %collective-permute-done.2.refs_2_), channel_id=1, source_target_pairs={{0,256},{1,769},{2,258},{3,771},{4,260},{5,773},{6,262},{7,775},{8... | collective-permute-start | bytes 589832 | tf_op jit(solution)/shard_map/ppermute | solution.py:267
  139.6 3.8 %collective-permute-start.6 = (bf16[32,3072]{1,0:T(8,128)(2,1)S(1)}, bf16[32,3072]{1,0:T(8,128)(2,1)S(1)}, u32[]{:S(2)}, u32[]{:S(2)}) collective-permute-start(bf16[32,3072]{1,0:T(8,128)(2,1)S(1)} %collective-permute-done.2.refs_2_), channel_id=1, source_target_pairs={{0,128},{1,897},{2,130},{3,899},{4,132},{5,901},{6,134},{7,903},{8... | collective-permute-start | bytes 589832 | tf_op jit(solution)/shard_map/ppermute | solution.py:267
  143.4 0.0 collective-permute-done.5.refs_5_
  143.4 0.0 collective-permute-done.4.refs_4_
  143.4 3.2 %collective-permute-done.7.refs_7_ = bf16[32,3072]{1,0:T(8,128)(2,1)S(1)} collective-permute-done((bf16[32,3072]{1,0:T(8,128)(2,1)S(1)}, bf16[32,3072]{1,0:T(8,128)(2,1)S(1)}, u32[]{:S(2)}, u32[]{:S(2)}) %collective-permute-start.7) | collective-permute-done | bytes 196640 | tf_op jit(solution)/shard_map/ppermute | solution.py:267
  146.6 0.0 collective-permute-done.8.refs_8_
  146.6 2.9 %collective-permute-done.6.refs_6_ = bf16[32,3072]{1,0:T(8,128)(2,1)S(1)} collective-permute-done((bf16[32,3072]{1,0:T(8,128)(2,1)S(1)}, bf16[32,3072]{1,0:T(8,128)(2,1)S(1)}, u32[]{:S(2)}, u32[]{:S(2)}) %collective-permute-start.6) | collective-permute-done | bytes 196640 | tf_op jit(solution)/shard_map/ppermute | solution.py:267
  149.5 0.6 shard_map.106
  150.1 15.6 %all_to_all.17 = bf16[64,8,128]{2,1,0:T(8,128)(2,1)S(1)} all-to-all(bf16[64,8,128]{2,1,0:T(8,128)(2,1)S(1)} %bitcast.32), channel_id=1, replica_groups=mesh['ep'=16,'edp'=64] {'edp'}, dimensions={0} | all-to-all | bytes 262144 | tf_op jit(solution)/shard_map/all_to_all | solution.py:289
  165.8 0.3 shard_map.107
  166.1 2.7 %collective-permute-start.9 = (bf16[64,128]{1,0:T(8,128)(2,1)S(1)}, bf16[64,128]{1,0:T(8,128)(2,1)S(1)}, u32[]{:S(2)}, u32[]{:S(2)}) collective-permute-start(bf16[64,128]{1,0:T(8,128)(2,1)S(1)} %shard_map.107), channel_id=1, source_target_pairs={{0,0},{1,1},{2,2},{3,3},{64,4},{65,5},{66,6},{67,7},{128,8},{129,9... | collective-permute-start | bytes 49160 | tf_op jit(solution)/shard_map/ppermute | solution.py:306
  168.7 1.5 shard_map.108
  170.2 10.8 %collective-permute-done.9 = bf16[64,128]{1,0:T(8,128)(2,1)S(1)} collective-permute-done((bf16[64,128]{1,0:T(8,128)(2,1)S(1)}, bf16[64,128]{1,0:T(8,128)(2,1)S(1)}, u32[]{:S(2)}, u32[]{:S(2)}) %collective-permute-start.9) | collective-permute-done | bytes 16416 | tf_op jit(solution)/shard_map/ppermute | solution.py:306
  181.0 0.6 copy.12
  (2 shorter events, 0.0 us)
Async XLA Ops:
  0.6 45.8 %copy-start.2 = (bf16[1,1024,256]{2,1,0:T(8,128)(2,1)S(1)}, bf16[1,1024,256]{2,1,0:T(8,128)(2,1)}, u32[]{:S(2)}) copy-start(bf16[1,1024,256]{2,1,0:T(8,128)(2,1)} %param.13) | copy-start | bytes 1572868
  0.6 45.7 %copy-start.1 = (bf16[1,256,1024]{2,1,0:T(8,128)(2,1)S(1)}, bf16[1,256,1024]{2,1,0:T(8,128)(2,1)}, u32[]{:S(2)}) copy-start(bf16[1,256,1024]{2,1,0:T(8,128)(2,1)} %param.12) | copy-start | bytes 1572868
  0.7 45.7 %copy-start = (bf16[1,256,1024]{2,1,0:T(8,128)(2,1)S(1)}, bf16[1,256,1024]{2,1,0:T(8,128)(2,1)}, u32[]{:S(2)}) copy-start(bf16[1,256,1024]{2,1,0:T(8,128)(2,1)} %param.11) | copy-start | bytes 1572868
  2.4 21.1 %collective-permute-start = (bf16[144,128]{1,0:T(8,128)(2,1)S(1)}, bf16[144,128]{1,0:T(8,128)(2,1)S(1)}, u32[]{:S(2)}, u32[]{:S(2)}) collective-permute-start(bf16[144,128]{1,0:T(8,128)(2,1)S(1)} %maximum_maximum_fusion), channel_id=1, source_target_pairs={{0,0},{1,1},{2,2},{3,3},{4,64},{5,65},{6,66},{7,67},{8,128},{9,129... | collective-permute-start | bytes 110600 | tf_op jit(solution)/shard_map/ppermute | solution.py:197
  47.7 58.2 %copy-start.3 = (f32[16,128]{1,0:T(8,128)S(1)}, f32[16,128]{1,0:T(8,128)}, u32[]{:S(2)}) copy-start(f32[16,128]{1,0:T(8,128)} %shard_map.102.weight_ref) | copy-start | bytes 24580
  106.3 12.2 %collective-permute-start.1 = (bf16[16,3072]{1,0:T(8,128)(2,1)S(1)}, bf16[16,3072]{1,0:T(8,128)(2,1)S(1)}, u32[]{:S(2)}, u32[]{:S(2)}) collective-permute-start(bf16[16,3072]{1,0:T(8,128)(2,1)S(1)} %shard_map.105), channel_id=1, source_target_pairs={{0,64},{64,0},{128,192},{192,128},{256,320},{320,256},{384,448},{4... | collective-permute-start | bytes 294920 | tf_op jit(solution)/shard_map/ppermute | solution.py:263
  118.5 15.9 %collective-permute-start.3 = (bf16[32,3072]{1,0:T(8,128)(2,1)S(1)}, bf16[32,3072]{1,0:T(8,128)(2,1)S(1)}, u32[]{:S(2)}, u32[]{:S(2)}) collective-permute-start(bf16[32,3072]{1,0:T(8,128)(2,1)S(1)} %pad_maximum_fusion.refs_1_), channel_id=1, source_target_pairs={{0,768},{1,257},{2,770},{3,259},{4,772},{5,261},{6,774},{7,263},{8... | collective-permute-start | bytes 589832 | tf_op jit(solution)/shard_map/ppermute | solution.py:267
  120.4 15.9 %collective-permute-start.2 = (bf16[32,3072]{1,0:T(8,128)(2,1)S(1)}, bf16[32,3072]{1,0:T(8,128)(2,1)S(1)}, u32[]{:S(2)}, u32[]{:S(2)}) collective-permute-start(bf16[32,3072]{1,0:T(8,128)(2,1)S(1)} %pad_maximum_fusion.refs_1_), channel_id=1, source_target_pairs={{0,256},{1,769},{2,258},{3,771},{4,260},{5,773},{6,262},{7,775},{8... | collective-permute-start | bytes 589832 | tf_op jit(solution)/shard_map/ppermute | solution.py:267
  126.5 16.9 %collective-permute-start.5 = (bf16[32,3072]{1,0:T(8,128)(2,1)S(1)}, bf16[32,3072]{1,0:T(8,128)(2,1)S(1)}, u32[]{:S(2)}, u32[]{:S(2)}) collective-permute-start(bf16[32,3072]{1,0:T(8,128)(2,1)S(1)} %pad_maximum_fusion.refs_1_), channel_id=1, source_target_pairs={{0,896},{1,129},{2,898},{3,131},{4,900},{5,133},{6,902},{7,135},{8... | collective-permute-start | bytes 589832 | tf_op jit(solution)/shard_map/ppermute | solution.py:267
  128.4 15.0 %collective-permute-start.4 = (bf16[32,3072]{1,0:T(8,128)(2,1)S(1)}, bf16[32,3072]{1,0:T(8,128)(2,1)S(1)}, u32[]{:S(2)}, u32[]{:S(2)}) collective-permute-start(bf16[32,3072]{1,0:T(8,128)(2,1)S(1)} %pad_maximum_fusion.refs_1_), channel_id=1, source_target_pairs={{0,128},{1,897},{2,130},{3,899},{4,132},{5,901},{6,134},{7,903},{8... | collective-permute-start | bytes 589832 | tf_op jit(solution)/shard_map/ppermute | solution.py:267
  134.4 12.2 %collective-permute-start.7 = (bf16[32,3072]{1,0:T(8,128)(2,1)S(1)}, bf16[32,3072]{1,0:T(8,128)(2,1)S(1)}, u32[]{:S(2)}, u32[]{:S(2)}) collective-permute-start(bf16[32,3072]{1,0:T(8,128)(2,1)S(1)} %collective-permute-done.3.refs_3_), channel_id=1, source_target_pairs={{0,896},{1,129},{2,898},{3,131},{4,900},{5,133},{6,902},{7,135},{8... | collective-permute-start | bytes 589832 | tf_op jit(solution)/shard_map/ppermute | solution.py:267
  136.3 10.3 %collective-permute-start.8 = (bf16[32,3072]{1,0:T(8,128)(2,1)S(1)}, bf16[32,3072]{1,0:T(8,128)(2,1)S(1)}, u32[]{:S(2)}, u32[]{:S(2)}) collective-permute-start(bf16[32,3072]{1,0:T(8,128)(2,1)S(1)} %collective-permute-done.2.refs_2_), channel_id=1, source_target_pairs={{0,256},{1,769},{2,258},{3,771},{4,260},{5,773},{6,262},{7,775},{8... | collective-permute-start | bytes 589832 | tf_op jit(solution)/shard_map/ppermute | solution.py:267
  139.6 9.9 %collective-permute-start.6 = (bf16[32,3072]{1,0:T(8,128)(2,1)S(1)}, bf16[32,3072]{1,0:T(8,128)(2,1)S(1)}, u32[]{:S(2)}, u32[]{:S(2)}) collective-permute-start(bf16[32,3072]{1,0:T(8,128)(2,1)S(1)} %collective-permute-done.2.refs_2_), channel_id=1, source_target_pairs={{0,128},{1,897},{2,130},{3,899},{4,132},{5,901},{6,134},{7,903},{8... | collective-permute-start | bytes 589832 | tf_op jit(solution)/shard_map/ppermute | solution.py:267
  166.1 14.9 %collective-permute-start.9 = (bf16[64,128]{1,0:T(8,128)(2,1)S(1)}, bf16[64,128]{1,0:T(8,128)(2,1)S(1)}, u32[]{:S(2)}, u32[]{:S(2)}) collective-permute-start(bf16[64,128]{1,0:T(8,128)(2,1)S(1)} %shard_map.107), channel_id=1, source_target_pairs={{0,0},{1,1},{2,2},{3,3},{64,4},{65,5},{66,6},{67,7},{128,8},{129,9... | collective-permute-start | bytes 49160 | tf_op jit(solution)/shard_map/ppermute | solution.py:306

commit v8 on v7

--- a/solution.py
+++ b/solution.py
@@ -122,10 +122,9 @@
     ring = sum(len(held) for held in steps)
     spot = lax.div(place_ref[0], 2 * experts)
     side = lax.rem(lax.div(place_ref[0], experts), 2)
-    way = 1 - 2 * lax.rem(place_ref[0], 2)
     for held, piece_ref in zip(steps, pieces, strict=True):
         for at, step in enumerate(held):
-            pair = 2 * CAP * lax.rem(spot + step * way + ring, ring)
+            pair = 2 * CAP * lax.rem(spot + step + ring, ring)
             for half, z in ((0, side), (1, 1 - side)):
                 row = pl.multiple_of(pair + CAP * z, CAP)
                 low = (2 * at + half) * CAP
@@ -254,7 +253,7 @@
         return [
             (
                 b * experts + e,
-                ((b // 2 + (step if e % 2 == 0 else -step)) % ring * 2 + b % 2) * experts + e,
+                ((b // 2 + step) % ring * 2 + b % 2) * experts + e,
             )
             for b in range(blocks)
             for e in range(experts)

time: 182 us -> 186 us (1.022)
  the two profiles are of different devices: /device:TPU:38 before, /device:TPU:10 now
where the time goes in v8:
time: 186 us; the launch traced here: 185 us
  blocking collectives  104 us (56%)
  starting transfers between devices  46.2 us (25%)
  waiting for transfers between devices  26 us (14%)
  Pallas kernels  5.87 us (3%)
    all_to_all x1, blocking collectives, per_device(): lax.all_to_all(part.reshape(blocks, CAP, 3 * hid), 'ep', split_axis=0, co...  56.3 us
    all_to_all x1, blocking collectives, per_device(): lax.all_to_all(sent.reshape(experts, CAP, 2 * width), 'edp', split_axis=0...  30.6 us
    ppermute x7, starting transfers between devices, passed(): return lax.ppermute(piece, ('ep', 'edp'), shifted(step))  24.8 us
    all_to_all x1, blocking collectives, per_device(): lax.all_to_all(slot_grad.reshape(experts, 8, 128), 'edp', split_axis=0, c...  16.7 us
    ppermute x1, starting transfers between devices, per_device(): packed = lax.ppermute(packed, ('ep', 'edp'), there)  13.5 us
    ppermute x7, waiting for transfers between devices, passed(): return lax.ppermute(piece, ('ep', 'edp'), shifted(step))  8.77 us
    ppermute x1, waiting for transfers between devices, per_device(): token_grad = lax.ppermute(token_grad, ('ep', 'edp'), back).T  8.32 us
    ppermute x1, waiting for transfers between devices, per_device(): other = lax.ppermute(mine, 'ep', [(b, b ^ 1) for b in range(blocks)])  8.2 us
  transfers between devices with their start and end apart: 10, of which 6 were waited for; matrix products, arithmetic and copies ran while one was open for 0% of the time, Pallas kernels for 2%

profile of v8, /device:TPU:10, one launch (start us, length us, event | category | flops | bytes accessed | tf_op | source)
XLA Modules:
  0.0 184.9 jit_solution(14022435243908001328)
XLA Ops:
  0.6 0.0 copy-start.2
  0.6 0.0 copy-start.1
  0.7 0.0 copy-start
  0.7 0.8 bitcast_convert_fusion
  1.5 0.1 pad.5.clone
  1.6 0.8 maximum_maximum_fusion
  2.4 13.5 %collective-permute-start = (bf16[144,128]{1,0:T(8,128)(2,1)S(1)}, bf16[144,128]{1,0:T(8,128)(2,1)S(1)}, u32[]{:S(2)}, u32[]{:S(2)}) collective-permute-start(bf16[144,128]{1,0:T(8,128)(2,1)S(1)} %maximum_maximum_fusion), channel_id=1, source_target_pairs={{0,0},{1,1},{2,2},{3,3},{4,64},{5,65},{6,66},{7,67},{8,128},{9,129... | collective-permute-start | bytes 110600 | tf_op jit(solution)/shard_map/ppermute | solution.py:196
  15.9 1.5 shard_map.102.weight_ref
  17.4 0.7 collective-permute-done.refs_0_
  18.1 0.4 shard_map.103
  18.5 30.6 %all_to_all.15 = bf16[64,16,128]{2,1,0:T(8,128)(2,1)S(1)} all-to-all(bf16[64,16,128]{2,1,0:T(8,128)(2,1)S(1)} %bitcast.31), channel_id=1, replica_groups=mesh['ep'=16,'edp'=64] {'edp'}, dimensions={0} | all-to-all | bytes 524288 | tf_op jit(solution)/shard_map/all_to_all | solution.py:224
  49.2 0.0 copy-done.2
  49.2 0.0 copy-done.1
  49.2 0.0 copy-done
  49.2 1.3 shard_map.104
  50.5 0.0 copy-start.3
  50.5 56.3 %all_to_all.16 = bf16[16,16,3072]{2,1,0:T(8,128)(2,1)S(1)} all-to-all(bf16[16,16,3072]{2,1,0:T(8,128)(2,1)S(1)} %bitcast.28), channel_id=1, replica_groups=mesh['ep'=16,'edp'=64] {'ep'}, dimensions={0} | all-to-all | bytes 3145728 | tf_op jit(solution)/shard_map/all_to_all | solution.py:244
  106.8 0.0 copy-done.3
  106.8 0.3 shard_map.105
  107.1 2.5 %collective-permute-start.1 = (bf16[16,3072]{1,0:T(8,128)(2,1)S(1)}, bf16[16,3072]{1,0:T(8,128)(2,1)S(1)}, u32[]{:S(2)}, u32[]{:S(2)}) collective-permute-start(bf16[16,3072]{1,0:T(8,128)(2,1)S(1)} %shard_map.105), channel_id=1, source_target_pairs={{0,64},{64,0},{128,192},{192,128},{256,320},{320,256},{384,448},{4... | collective-permute-start | bytes 294920 | tf_op jit(solution)/shard_map/ppermute | solution.py:262
  109.6 8.2 %collective-permute-done.1 = bf16[16,3072]{1,0:T(8,128)(2,1)S(1)} collective-permute-done((bf16[16,3072]{1,0:T(8,128)(2,1)S(1)}, bf16[16,3072]{1,0:T(8,128)(2,1)S(1)}, u32[]{:S(2)}, u32[]{:S(2)}) %collective-permute-start.1) | collective-permute-done | bytes 98336 | tf_op jit(solution)/shard_map/ppermute | solution.py:262
  117.8 5.2 %collective-permute-start.3 = (bf16[32,3072]{1,0:T(8,128)(2,1)S(1)}, bf16[32,3072]{1,0:T(8,128)(2,1)S(1)}, u32[]{:S(2)}, u32[]{:S(2)}) collective-permute-start(bf16[32,3072]{1,0:T(8,128)(2,1)S(1)} %pad_maximum_fusion.refs_1_), channel_id=1, source_target_pairs={{0,768},{1,769},{2,770},{3,771},{4,772},{5,773},{6,774},{7,775},{8... | collective-permute-start | bytes 589832 | tf_op jit(solution)/shard_map/ppermute | solution.py:266
  123.0 1.9 %collective-permute-start.2 = (bf16[32,3072]{1,0:T(8,128)(2,1)S(1)}, bf16[32,3072]{1,0:T(8,128)(2,1)S(1)}, u32[]{:S(2)}, u32[]{:S(2)}) collective-permute-start(bf16[32,3072]{1,0:T(8,128)(2,1)S(1)} %pad_maximum_fusion.refs_1_), channel_id=1, source_target_pairs={{0,256},{1,257},{2,258},{3,259},{4,260},{5,261},{6,262},{7,263},{8... | collective-permute-start | bytes 589832 | tf_op jit(solution)/shard_map/ppermute | solution.py:266
  125.0 4.7 %collective-permute-start.5 = (bf16[32,3072]{1,0:T(8,128)(2,1)S(1)}, bf16[32,3072]{1,0:T(8,128)(2,1)S(1)}, u32[]{:S(2)}, u32[]{:S(2)}) collective-permute-start(bf16[32,3072]{1,0:T(8,128)(2,1)S(1)} %pad_maximum_fusion.refs_1_), channel_id=1, source_target_pairs={{0,896},{1,897},{2,898},{3,899},{4,900},{5,901},{6,902},{7,903},{8... | collective-permute-start | bytes 589832 | tf_op jit(solution)/shard_map/ppermute | solution.py:266
  129.7 1.9 %collective-permute-start.4 = (bf16[32,3072]{1,0:T(8,128)(2,1)S(1)}, bf16[32,3072]{1,0:T(8,128)(2,1)S(1)}, u32[]{:S(2)}, u32[]{:S(2)}) collective-permute-start(bf16[32,3072]{1,0:T(8,128)(2,1)S(1)} %pad_maximum_fusion.refs_1_), channel_id=1, source_target_pairs={{0,128},{1,129},{2,130},{3,131},{4,132},{5,133},{6,134},{7,135},{8... | collective-permute-start | bytes 589832 | tf_op jit(solution)/shard_map/ppermute | solution.py:266
  131.6 0.0 collective-permute-done.3.refs_3_
  131.6 3.9 %collective-permute-start.7 = (bf16[32,3072]{1,0:T(8,128)(2,1)S(1)}, bf16[32,3072]{1,0:T(8,128)(2,1)S(1)}, u32[]{:S(2)}, u32[]{:S(2)}) collective-permute-start(bf16[32,3072]{1,0:T(8,128)(2,1)S(1)} %collective-permute-done.3.refs_3_), channel_id=1, source_target_pairs={{0,896},{1,897},{2,898},{3,899},{4,900},{5,901},{6,902},{7,903},{8... | collective-permute-start | bytes 589832 | tf_op jit(solution)/shard_map/ppermute | solution.py:266
  135.5 0.8 collective-permute-done.2.refs_2_
  136.3 2.0 %collective-permute-start.8 = (bf16[32,3072]{1,0:T(8,128)(2,1)S(1)}, bf16[32,3072]{1,0:T(8,128)(2,1)S(1)}, u32[]{:S(2)}, u32[]{:S(2)}) collective-permute-start(bf16[32,3072]{1,0:T(8,128)(2,1)S(1)} %collective-permute-done.2.refs_2_), channel_id=1, source_target_pairs={{0,256},{1,257},{2,258},{3,259},{4,260},{5,261},{6,262},{7,263},{8... | collective-permute-start | bytes 589832 | tf_op jit(solution)/shard_map/ppermute | solution.py:266
  138.3 5.1 %collective-permute-start.6 = (bf16[32,3072]{1,0:T(8,128)(2,1)S(1)}, bf16[32,3072]{1,0:T(8,128)(2,1)S(1)}, u32[]{:S(2)}, u32[]{:S(2)}) collective-permute-start(bf16[32,3072]{1,0:T(8,128)(2,1)S(1)} %collective-permute-done.2.refs_2_), channel_id=1, source_target_pairs={{0,128},{1,129},{2,130},{3,131},{4,132},{5,133},{6,134},{7,135},{8... | collective-permute-start | bytes 589832 | tf_op jit(solution)/shard_map/ppermute | solution.py:266
  143.4 0.0 collective-permute-done.5.refs_5_
  143.4 0.0 collective-permute-done.4.refs_4_
  143.5 0.0 collective-permute-done.7.refs_7_
  143.5 7.0 %collective-permute-done.8.refs_8_ = bf16[32,3072]{1,0:T(8,128)(2,1)S(1)} collective-permute-done((bf16[32,3072]{1,0:T(8,128)(2,1)S(1)}, bf16[32,3072]{1,0:T(8,128)(2,1)S(1)}, u32[]{:S(2)}, u32[]{:S(2)}) %collective-permute-start.8) | collective-permute-done | bytes 196640 | tf_op jit(solution)/shard_map/ppermute | solution.py:266
  150.4 1.0 collective-permute-done.6.refs_6_
  151.4 0.6 shard_map.106
  152.1 16.7 %all_to_all.17 = bf16[64,8,128]{2,1,0:T(8,128)(2,1)S(1)} all-to-all(bf16[64,8,128]{2,1,0:T(8,128)(2,1)S(1)} %bitcast.32), channel_id=1, replica_groups=mesh['ep'=16,'edp'=64] {'edp'}, dimensions={0} | all-to-all | bytes 262144 | tf_op jit(solution)/shard_map/all_to_all | solution.py:288
  168.7 0.3 shard_map.107
  169.0 5.4 %collective-permute-start.9 = (bf16[64,128]{1,0:T(8,128)(2,1)S(1)}, bf16[64,128]{1,0:T(8,128)(2,1)S(1)}, u32[]{:S(2)}, u32[]{:S(2)}) collective-permute-start(bf16[64,128]{1,0:T(8,128)(2,1)S(1)} %shard_map.107), channel_id=1, source_target_pairs={{0,0},{1,1},{2,2},{3,3},{64,4},{65,5},{66,6},{67,7},{128,8},{129,9... | collective-permute-start | bytes 49160 | tf_op jit(solution)/shard_map/ppermute | solution.py:305
  174.5 1.5 shard_map.108
  175.9 8.3 %collective-permute-done.9 = bf16[64,128]{1,0:T(8,128)(2,1)S(1)} collective-permute-done((bf16[64,128]{1,0:T(8,128)(2,1)S(1)}, bf16[64,128]{1,0:T(8,128)(2,1)S(1)}, u32[]{:S(2)}, u32[]{:S(2)}) %collective-permute-start.9) | collective-permute-done | bytes 16416 | tf_op jit(solution)/shard_map/ppermute | solution.py:305
  184.3 0.6 copy.12
  (2 shorter events, 0.0 us)
Async XLA Ops:
  0.6 48.5 %copy-start.2 = (bf16[1,1024,256]{2,1,0:T(8,128)(2,1)S(1)}, bf16[1,1024,256]{2,1,0:T(8,128)(2,1)}, u32[]{:S(2)}) copy-start(bf16[1,1024,256]{2,1,0:T(8,128)(2,1)} %param.13) | copy-start | bytes 1572868
  0.6 48.5 %copy-start.1 = (bf16[1,256,1024]{2,1,0:T(8,128)(2,1)S(1)}, bf16[1,256,1024]{2,1,0:T(8,128)(2,1)}, u32[]{:S(2)}) copy-start(bf16[1,256,1024]{2,1,0:T(8,128)(2,1)} %param.12) | copy-start | bytes 1572868
  0.7 48.5 %copy-start = (bf16[1,256,1024]{2,1,0:T(8,128)(2,1)S(1)}, bf16[1,256,1024]{2,1,0:T(8,128)(2,1)}, u32[]{:S(2)}) copy-start(bf16[1,256,1024]{2,1,0:T(8,128)(2,1)} %param.11) | copy-start | bytes 1572868
  2.4 15.8 %collective-permute-start = (bf16[144,128]{1,0:T(8,128)(2,1)S(1)}, bf16[144,128]{1,0:T(8,128)(2,1)S(1)}, u32[]{:S(2)}, u32[]{:S(2)}) collective-permute-start(bf16[144,128]{1,0:T(8,128)(2,1)S(1)} %maximum_maximum_fusion), channel_id=1, source_target_pairs={{0,0},{1,1},{2,2},{3,3},{4,64},{5,65},{6,66},{7,67},{8,128},{9,129... | collective-permute-start | bytes 110600 | tf_op jit(solution)/shard_map/ppermute | solution.py:196
  50.5 56.3 %copy-start.3 = (f32[16,128]{1,0:T(8,128)S(1)}, f32[16,128]{1,0:T(8,128)}, u32[]{:S(2)}) copy-start(f32[16,128]{1,0:T(8,128)} %shard_map.102.weight_ref) | copy-start | bytes 24580
  107.1 10.7 %collective-permute-start.1 = (bf16[16,3072]{1,0:T(8,128)(2,1)S(1)}, bf16[16,3072]{1,0:T(8,128)(2,1)S(1)}, u32[]{:S(2)}, u32[]{:S(2)}) collective-permute-start(bf16[16,3072]{1,0:T(8,128)(2,1)S(1)} %shard_map.105), channel_id=1, source_target_pairs={{0,64},{64,0},{128,192},{192,128},{256,320},{320,256},{384,448},{4... | collective-permute-start | bytes 294920 | tf_op jit(solution)/shard_map/ppermute | solution.py:262
  117.8 13.8 %collective-permute-start.3 = (bf16[32,3072]{1,0:T(8,128)(2,1)S(1)}, bf16[32,3072]{1,0:T(8,128)(2,1)S(1)}, u32[]{:S(2)}, u32[]{:S(2)}) collective-permute-start(bf16[32,3072]{1,0:T(8,128)(2,1)S(1)} %pad_maximum_fusion.refs_1_), channel_id=1, source_target_pairs={{0,768},{1,769},{2,770},{3,771},{4,772},{5,773},{6,774},{7,775},{8... | collective-permute-start | bytes 589832 | tf_op jit(solution)/shard_map/ppermute | solution.py:266
  123.0 13.3 %collective-permute-start.2 = (bf16[32,3072]{1,0:T(8,128)(2,1)S(1)}, bf16[32,3072]{1,0:T(8,128)(2,1)S(1)}, u32[]{:S(2)}, u32[]{:S(2)}) collective-permute-start(bf16[32,3072]{1,0:T(8,128)(2,1)S(1)} %pad_maximum_fusion.refs_1_), channel_id=1, source_target_pairs={{0,256},{1,257},{2,258},{3,259},{4,260},{5,261},{6,262},{7,263},{8... | collective-permute-start | bytes 589832 | tf_op jit(solution)/shard_map/ppermute | solution.py:266
  125.0 18.5 %collective-permute-start.5 = (bf16[32,3072]{1,0:T(8,128)(2,1)S(1)}, bf16[32,3072]{1,0:T(8,128)(2,1)S(1)}, u32[]{:S(2)}, u32[]{:S(2)}) collective-permute-start(bf16[32,3072]{1,0:T(8,128)(2,1)S(1)} %pad_maximum_fusion.refs_1_), channel_id=1, source_target_pairs={{0,896},{1,897},{2,898},{3,899},{4,900},{5,901},{6,902},{7,903},{8... | collective-permute-start | bytes 589832 | tf_op jit(solution)/shard_map/ppermute | solution.py:266
  129.7 13.8 %collective-permute-start.4 = (bf16[32,3072]{1,0:T(8,128)(2,1)S(1)}, bf16[32,3072]{1,0:T(8,128)(2,1)S(1)}, u32[]{:S(2)}, u32[]{:S(2)}) collective-permute-start(bf16[32,3072]{1,0:T(8,128)(2,1)S(1)} %pad_maximum_fusion.refs_1_), channel_id=1, source_target_pairs={{0,128},{1,129},{2,130},{3,131},{4,132},{5,133},{6,134},{7,135},{8... | collective-permute-start | bytes 589832 | tf_op jit(solution)/shard_map/ppermute | solution.py:266
  131.6 11.9 %collective-permute-start.7 = (bf16[32,3072]{1,0:T(8,128)(2,1)S(1)}, bf16[32,3072]{1,0:T(8,128)(2,1)S(1)}, u32[]{:S(2)}, u32[]{:S(2)}) collective-permute-start(bf16[32,3072]{1,0:T(8,128)(2,1)S(1)} %collective-permute-done.3.refs_3_), channel_id=1, source_target_pairs={{0,896},{1,897},{2,898},{3,899},{4,900},{5,901},{6,902},{7,903},{8... | collective-permute-start | bytes 589832 | tf_op jit(solution)/shard_map/ppermute | solution.py:266
  136.3 14.1 %collective-permute-start.8 = (bf16[32,3072]{1,0:T(8,128)(2,1)S(1)}, bf16[32,3072]{1,0:T(8,128)(2,1)S(1)}, u32[]{:S(2)}, u32[]{:S(2)}) collective-permute-start(bf16[32,3072]{1,0:T(8,128)(2,1)S(1)} %collective-permute-done.2.refs_2_), channel_id=1, source_target_pairs={{0,256},{1,257},{2,258},{3,259},{4,260},{5,261},{6,262},{7,263},{8... | collective-permute-start | bytes 589832 | tf_op jit(solution)/shard_map/ppermute | solution.py:266
  138.3 13.2 %collective-permute-start.6 = (bf16[32,3072]{1,0:T(8,128)(2,1)S(1)}, bf16[32,3072]{1,0:T(8,128)(2,1)S(1)}, u32[]{:S(2)}, u32[]{:S(2)}) collective-permute-start(bf16[32,3072]{1,0:T(8,128)(2,1)S(1)} %collective-permute-done.2.refs_2_), channel_id=1, source_target_pairs={{0,128},{1,129},{2,130},{3,131},{4,132},{5,133},{6,134},{7,135},{8... | collective-permute-start | bytes 589832 | tf_op jit(solution)/shard_map/ppermute | solution.py:266
  169.0 15.2 %collective-permute-start.9 = (bf16[64,128]{1,0:T(8,128)(2,1)S(1)}, bf16[64,128]{1,0:T(8,128)(2,1)S(1)}, u32[]{:S(2)}, u32[]{:S(2)}) collective-permute-start(bf16[64,128]{1,0:T(8,128)(2,1)S(1)} %shard_map.107), channel_id=1, source_target_pairs={{0,0},{1,1},{2,2},{3,3},{64,4},{65,5},{66,6},{67,7},{128,8},{129,9... | collective-permute-start | bytes 49160 | tf_op jit(solution)/shard_map/ppermute | solution.py:305
